TPU v7x, 256 devices: a whole 4x4x8 slice. The times are simulated.
256 devices in a mesh: region: 8 (over x, core), dom: 32 (over y, z).
Axes of the slice: x: 4, y: 4, z: 8, core: 2. Of those that a mesh axis runs over, the one named last changes fastest.
Arguments:
- inputs: bfloat16 [131072, 512], P(('region', 'dom')), may hold values from -6 to 6
- state_init: bfloat16 [131072, 128], P(('region', 'dom')), may hold values from -6 to 6
- neighbors: int32 [131072, 4], P(('region', 'dom')), may hold values from 0 to 575
- edge_weight: float32 [131072, 4], P(('region', 'dom')), may hold values from 0.1 to 1
- boundary: int32 [16384], P(('region', 'dom')), may hold values from 0 to 511
- w_gate: bfloat16 [3, 256, 256], replicated, may hold values from -1 to 1
- b_gate: float32 [256], replicated, may hold values from -3 to 3
- w_cand: bfloat16 [3, 256, 128], replicated, may hold values from -0.4375 to 0.4375
- b_cand: float32 [128], replicated, may hold values from -3 to 3
- w_out: bfloat16 [128, 128], replicated, may hold values from -0.5 to 0.5
- b_out: float32 [128], replicated, may hold values from -4 to 4
- inc_block: int32 [262144], P(('region', 'dom')), may hold values from 0 to 31
- inc_path: int32 [262144], P(('region', 'dom')), may hold values from 0 to 2047
- path_slot: int32 [32, 2048], P('dom'), may hold values from 0 to 2047, each once within a row
Outputs:
- state_final: bfloat16 [131072, 128], P(('region', 'dom'))
- path_times: float32 [32, 2048, 128], P('dom', 'region')
Inputs may be any that keep to these rules, and one draw needn't show every extreme that they name: `path_slot`: each row is a permutation of 0 to 2047.
All inputs are finite; a program needn't handle non-finite values.
Results may differ from a plain program's by a relative error of at most 0.011.
Values may be sent and summed in bfloat16 or wider, within the bound.
A program may use at most 64 MiB of HBM per device.

v0:
```python
import jax
import jax.numpy as jnp
from jax import lax
from jax.sharding import PartitionSpec as P

BS = 16


def extended_2(array, sides, width):
    for axis, dim in sides:
        peers, length = (lax.axis_size(axis), array.shape[dim])
        up = [(i, (i + 1) % peers) for i in range(peers - 1)]
        down = [(j, i) for i, j in up]
        last = lax.slice_in_dim(array, length - width, length, axis=dim)
        leading = lax.slice_in_dim(array, 0, width, axis=dim)
        before = lax.ppermute(last, axis, up)
        after = lax.ppermute(leading, axis, down)
        array = jnp.concatenate([before, array, after], axis=dim)
    return array


def extend(field, picker_edges):
    half = picker_edges.shape[0] // 2
    edges = jnp.dot(picker_edges, field, preferred_element_type=jnp.float32).astype(jnp.bfloat16)
    padded = extended_2(edges, (("dom", 0),), half)
    return jnp.concatenate([field, padded[:half], padded[-half:]], axis=0)


def spread(table, rows, picker_rows, weights):
    degree = weights.shape[1]
    picked = jnp.dot(picker_rows, table, preferred_element_type=jnp.float32).reshape(
        degree, rows, table.shape[1]
    )
    acc = jnp.zeros((rows, table.shape[1]), jnp.float32)
    for k in range(degree):
        acc = acc + weights[:, k : k + 1] * picked[k]
    return acc.astype(jnp.bfloat16)


def project(parts, weight, bias):
    stacked = jnp.concatenate(parts, axis=1)
    return (
        jnp.dot(stacked, weight.reshape(-1, weight.shape[-1]), preferred_element_type=jnp.float32)
        + bias
    )


def per_device(
    inputs,
    state_init,
    neighbors,
    edge_weight,
    boundary,
    w_gate,
    b_gate,
    w_cand,
    b_cand,
    w_out,
    b_out,
    inc_block,
    inc_path,
    path_slot,
):
    rows = inputs.shape[0]
    width_in = w_gate.shape[1] - state_init.shape[1]
    hidden = state_init.shape[1]
    lags = inputs.shape[1] // width_in
    weights = edge_weight / jnp.sum(edge_weight, axis=1, keepdims=True)
    extended = rows + boundary.shape[0]
    columns = jnp.arange(extended, dtype=jnp.int32)
    picker_rows = (jnp.transpose(neighbors)[:, :, None] == columns[None, None, :]).astype(
        jnp.bfloat16
    )
    picker_rows = picker_rows.reshape(-1, extended)
    local_cols = jnp.arange(rows, dtype=jnp.int32)
    picker_edges = (boundary[:, None] == local_cols[None, :]).astype(jnp.bfloat16)

    def diffuse(field):
        return spread(extend(field, picker_edges), rows, picker_rows, weights)

    h = state_init.astype(jnp.float32)
    for t in range(lags):
        x_t = inputs[:, t * width_in : (t + 1) * width_in]
        h_low = h.astype(jnp.bfloat16)
        z = jnp.concatenate([x_t, h_low], axis=1)
        s1 = diffuse(z)
        s2 = diffuse(s1)
        gates = project([z, s1, s2], w_gate, b_gate)
        reset = jax.nn.sigmoid(gates[:, :hidden])
        update = jax.nn.sigmoid(gates[:, hidden:])
        reset_state = (reset * h).astype(jnp.bfloat16)
        zc = jnp.concatenate([x_t, reset_state], axis=1)
        c1 = diffuse(zc)
        c2 = diffuse(c1)
        cand = jnp.tanh(project([zc, c1, c2], w_cand, b_cand))
        h = update * h + (1.0 - update) * cand
    state_final = h.astype(jnp.bfloat16)
    seg_time = 0.05 * jax.nn.softplus(
        jnp.dot(state_final, w_out, preferred_element_type=jnp.float32) + b_out
    )
    slots_out = w_out.shape[1]
    block_time = seg_time.reshape(rows // BS, BS, slots_out).sum(axis=1).astype(jnp.bfloat16)
    slots = jnp.take(path_slot[0], inc_path)
    paths_col = path_slot.shape[1]
    vals = jnp.take(block_time, inc_block, axis=0).astype(jnp.float32)
    partial_paths = jax.ops.segment_sum(vals, slots, num_segments=paths_col)
    owned = lax.psum_scatter(
        partial_paths.astype(jnp.bfloat16), "region", scatter_dimension=0, tiled=True
    ).astype(jnp.float32)
    return (state_final, owned[None])


def solution(mesh):
    placed = (
        P(("region", "dom"), None),
        P(("region", "dom"), None),
        P(("region", "dom"), None),
        P(("region", "dom"), None),
        P(("region", "dom")),
        P(),
        P(),
        P(),
        P(),
        P(),
        P(),
        P(("region", "dom")),
        P(("region", "dom")),
        P("dom", None),
    )
    return jax.shard_map(
        per_device,
        mesh=mesh,
        in_specs=placed,
        out_specs=(P(("region", "dom"), None), P("dom", "region", None)),
        check_vma=False,
    )
```

profile of v0, /device:TPU:25, one launch (start us, length us, event | category | flops | bytes accessed | tf_op | source)
XLA Modules:
  0.0 254.7 jit_solution(5814319566949627157)
XLA Ops:
  9.6 7.7 %collective-permute-start.1 = (bf16[32,256]{1,0:T(8,128)(2,1)S(1)}, bf16[32,256]{1,0:T(8,128)(2,1)S(1)}, u32[]{:S(2)}, u32[]{:S(2)}) collective-permute-start(bf16[32,256]{1,0:T(8,128)(2,1)S(1)} %get-tuple-element.37), channel_id=1, source_target_pairs={{1,0},{2,1},{3,2},{4,3},{5,4},{6,5},{7,6},{8,7},{9,8},{10,9},{11,1... | collective-permute-start | bytes 49160 | tf_op jit(solution)/shard_map/ppermute | solution.py:17
  17.3 1.9 collective-permute-start
  19.3 4.6 %collective-permute-done = bf16[32,256]{1,0:T(8,128)(2,1)S(1)} collective-permute-done((bf16[32,256]{1,0:T(8,128)(2,1)S(1)}, bf16[32,256]{1,0:T(8,128)(2,1)S(1)}, u32[]{:S(2)}, u32[]{:S(2)}) %collective-permute-start) | collective-permute-done | bytes 16416 | tf_op jit(solution)/shard_map/ppermute | solution.py:16
  26.0 1.9 collective-permute-start.3
  27.9 3.4 %collective-permute-start.2 = (bf16[32,256]{1,0:T(8,128)(2,1)S(1)}, bf16[32,256]{1,0:T(8,128)(2,1)S(1)}, u32[]{:S(2)}, u32[]{:S(2)}) collective-permute-start(bf16[32,256]{1,0:T(8,128)(2,1)S(1)} %get-tuple-element.34), channel_id=1, source_target_pairs={{0,1},{1,2},{2,3},{3,4},{4,5},{5,6},{6,7},{7,8},{8,9},{9,10},{10,1... | collective-permute-start | bytes 49160 | tf_op jit(solution)/shard_map/ppermute | solution.py:16
  31.3 3.2 %collective-permute-done.2 = bf16[32,256]{1,0:T(8,128)(2,1)S(1)} collective-permute-done((bf16[32,256]{1,0:T(8,128)(2,1)S(1)}, bf16[32,256]{1,0:T(8,128)(2,1)S(1)}, u32[]{:S(2)}, u32[]{:S(2)}) %collective-permute-start.2) | collective-permute-done | bytes 16416 | tf_op jit(solution)/shard_map/ppermute | solution.py:16
  37.1 1.9 collective-permute-start.5
  39.0 3.4 %collective-permute-start.4 = (bf16[32,256]{1,0:T(8,128)(2,1)S(1)}, bf16[32,256]{1,0:T(8,128)(2,1)S(1)}, u32[]{:S(2)}, u32[]{:S(2)}) collective-permute-start(bf16[32,256]{1,0:T(8,128)(2,1)S(1)} %get-tuple-element.32), channel_id=1, source_target_pairs={{0,1},{1,2},{2,3},{3,4},{4,5},{5,6},{6,7},{7,8},{8,9},{9,10},{10,1... | collective-permute-start | bytes 49160 | tf_op jit(solution)/shard_map/ppermute | solution.py:16
  42.4 3.2 %collective-permute-done.4 = bf16[32,256]{1,0:T(8,128)(2,1)S(1)} collective-permute-done((bf16[32,256]{1,0:T(8,128)(2,1)S(1)}, bf16[32,256]{1,0:T(8,128)(2,1)S(1)}, u32[]{:S(2)}, u32[]{:S(2)}) %collective-permute-start.4) | collective-permute-done | bytes 16416 | tf_op jit(solution)/shard_map/ppermute | solution.py:16
  47.4 1.9 collective-permute-start.7
  49.3 3.4 %collective-permute-start.6 = (bf16[32,256]{1,0:T(8,128)(2,1)S(1)}, bf16[32,256]{1,0:T(8,128)(2,1)S(1)}, u32[]{:S(2)}, u32[]{:S(2)}) collective-permute-start(bf16[32,256]{1,0:T(8,128)(2,1)S(1)} %get-tuple-element.30), channel_id=1, source_target_pairs={{0,1},{1,2},{2,3},{3,4},{4,5},{5,6},{6,7},{7,8},{8,9},{9,10},{10,1... | collective-permute-start | bytes 49160 | tf_op jit(solution)/shard_map/ppermute | solution.py:16
  52.7 3.2 %collective-permute-done.6 = bf16[32,256]{1,0:T(8,128)(2,1)S(1)} collective-permute-done((bf16[32,256]{1,0:T(8,128)(2,1)S(1)}, bf16[32,256]{1,0:T(8,128)(2,1)S(1)}, u32[]{:S(2)}, u32[]{:S(2)}) %collective-permute-start.6) | collective-permute-done | bytes 16416 | tf_op jit(solution)/shard_map/ppermute | solution.py:16
  58.6 1.9 collective-permute-start.9
  60.6 3.4 %collective-permute-start.8 = (bf16[32,256]{1,0:T(8,128)(2,1)S(1)}, bf16[32,256]{1,0:T(8,128)(2,1)S(1)}, u32[]{:S(2)}, u32[]{:S(2)}) collective-permute-start(bf16[32,256]{1,0:T(8,128)(2,1)S(1)} %get-tuple-element.28), channel_id=1, source_target_pairs={{0,1},{1,2},{2,3},{3,4},{4,5},{5,6},{6,7},{7,8},{8,9},{9,10},{10,1... | collective-permute-start | bytes 49160 | tf_op jit(solution)/shard_map/ppermute | solution.py:16
  63.9 3.2 %collective-permute-done.8 = bf16[32,256]{1,0:T(8,128)(2,1)S(1)} collective-permute-done((bf16[32,256]{1,0:T(8,128)(2,1)S(1)}, bf16[32,256]{1,0:T(8,128)(2,1)S(1)}, u32[]{:S(2)}, u32[]{:S(2)}) %collective-permute-start.8) | collective-permute-done | bytes 16416 | tf_op jit(solution)/shard_map/ppermute | solution.py:16
  68.9 1.9 collective-permute-start.11
  70.9 3.5 %collective-permute-start.10 = (bf16[32,256]{1,0:T(8,128)(2,1)S(1)}, bf16[32,256]{1,0:T(8,128)(2,1)S(1)}, u32[]{:S(2)}, u32[]{:S(2)}) collective-permute-start(bf16[32,256]{1,0:T(8,128)(2,1)S(1)} %get-tuple-element.26), channel_id=1, source_target_pairs={{0,1},{1,2},{2,3},{3,4},{4,5},{5,6},{6,7},{7,8},{8,9},{9,10},{10,1... | collective-permute-start | bytes 49160 | tf_op jit(solution)/shard_map/ppermute | solution.py:16
  74.4 3.0 %collective-permute-done.10 = bf16[32,256]{1,0:T(8,128)(2,1)S(1)} collective-permute-done((bf16[32,256]{1,0:T(8,128)(2,1)S(1)}, bf16[32,256]{1,0:T(8,128)(2,1)S(1)}, u32[]{:S(2)}, u32[]{:S(2)}) %collective-permute-start.10) | collective-permute-done | bytes 16416 | tf_op jit(solution)/shard_map/ppermute | solution.py:16
  79.7 1.9 collective-permute-start.13
  81.6 3.4 %collective-permute-start.12 = (bf16[32,256]{1,0:T(8,128)(2,1)S(1)}, bf16[32,256]{1,0:T(8,128)(2,1)S(1)}, u32[]{:S(2)}, u32[]{:S(2)}) collective-permute-start(bf16[32,256]{1,0:T(8,128)(2,1)S(1)} %get-tuple-element.24), channel_id=1, source_target_pairs={{0,1},{1,2},{2,3},{3,4},{4,5},{5,6},{6,7},{7,8},{8,9},{9,10},{10,1... | collective-permute-start | bytes 49160 | tf_op jit(solution)/shard_map/ppermute | solution.py:16
  85.0 3.2 %collective-permute-done.12 = bf16[32,256]{1,0:T(8,128)(2,1)S(1)} collective-permute-done((bf16[32,256]{1,0:T(8,128)(2,1)S(1)}, bf16[32,256]{1,0:T(8,128)(2,1)S(1)}, u32[]{:S(2)}, u32[]{:S(2)}) %collective-permute-start.12) | collective-permute-done | bytes 16416 | tf_op jit(solution)/shard_map/ppermute | solution.py:16
  90.0 1.9 collective-permute-start.15
  91.9 3.4 %collective-permute-start.14 = (bf16[32,256]{1,0:T(8,128)(2,1)S(1)}, bf16[32,256]{1,0:T(8,128)(2,1)S(1)}, u32[]{:S(2)}, u32[]{:S(2)}) collective-permute-start(bf16[32,256]{1,0:T(8,128)(2,1)S(1)} %get-tuple-element.22), channel_id=1, source_target_pairs={{0,1},{1,2},{2,3},{3,4},{4,5},{5,6},{6,7},{7,8},{8,9},{9,10},{10,1... | collective-permute-start | bytes 49160 | tf_op jit(solution)/shard_map/ppermute | solution.py:16
  95.3 3.2 %collective-permute-done.14 = bf16[32,256]{1,0:T(8,128)(2,1)S(1)} collective-permute-done((bf16[32,256]{1,0:T(8,128)(2,1)S(1)}, bf16[32,256]{1,0:T(8,128)(2,1)S(1)}, u32[]{:S(2)}, u32[]{:S(2)}) %collective-permute-start.14) | collective-permute-done | bytes 16416 | tf_op jit(solution)/shard_map/ppermute | solution.py:16
  100.7 1.9 collective-permute-start.17
  102.6 3.4 %collective-permute-start.16 = (bf16[32,256]{1,0:T(8,128)(2,1)S(1)}, bf16[32,256]{1,0:T(8,128)(2,1)S(1)}, u32[]{:S(2)}, u32[]{:S(2)}) collective-permute-start(bf16[32,256]{1,0:T(8,128)(2,1)S(1)} %get-tuple-element.20), channel_id=1, source_target_pairs={{0,1},{1,2},{2,3},{3,4},{4,5},{5,6},{6,7},{7,8},{8,9},{9,10},{10,1... | collective-permute-start | bytes 49160 | tf_op jit(solution)/shard_map/ppermute | solution.py:16
  106.0 3.2 %collective-permute-done.16 = bf16[32,256]{1,0:T(8,128)(2,1)S(1)} collective-permute-done((bf16[32,256]{1,0:T(8,128)(2,1)S(1)}, bf16[32,256]{1,0:T(8,128)(2,1)S(1)}, u32[]{:S(2)}, u32[]{:S(2)}) %collective-permute-start.16) | collective-permute-done | bytes 16416 | tf_op jit(solution)/shard_map/ppermute | solution.py:16
  111.0 1.9 collective-permute-start.19
  112.9 3.4 %collective-permute-start.18 = (bf16[32,256]{1,0:T(8,128)(2,1)S(1)}, bf16[32,256]{1,0:T(8,128)(2,1)S(1)}, u32[]{:S(2)}, u32[]{:S(2)}) collective-permute-start(bf16[32,256]{1,0:T(8,128)(2,1)S(1)} %get-tuple-element.18), channel_id=1, source_target_pairs={{0,1},{1,2},{2,3},{3,4},{4,5},{5,6},{6,7},{7,8},{8,9},{9,10},{10,1... | collective-permute-start | bytes 49160 | tf_op jit(solution)/shard_map/ppermute | solution.py:16
  116.3 3.2 %collective-permute-done.18 = bf16[32,256]{1,0:T(8,128)(2,1)S(1)} collective-permute-done((bf16[32,256]{1,0:T(8,128)(2,1)S(1)}, bf16[32,256]{1,0:T(8,128)(2,1)S(1)}, u32[]{:S(2)}, u32[]{:S(2)}) %collective-permute-start.18) | collective-permute-done | bytes 16416 | tf_op jit(solution)/shard_map/ppermute | solution.py:16
  121.8 1.9 collective-permute-start.21
  123.7 3.4 %collective-permute-start.20 = (bf16[32,256]{1,0:T(8,128)(2,1)S(1)}, bf16[32,256]{1,0:T(8,128)(2,1)S(1)}, u32[]{:S(2)}, u32[]{:S(2)}) collective-permute-start(bf16[32,256]{1,0:T(8,128)(2,1)S(1)} %get-tuple-element.16), channel_id=1, source_target_pairs={{0,1},{1,2},{2,3},{3,4},{4,5},{5,6},{6,7},{7,8},{8,9},{9,10},{10,1... | collective-permute-start | bytes 49160 | tf_op jit(solution)/shard_map/ppermute | solution.py:16
  127.1 3.2 %collective-permute-done.20 = bf16[32,256]{1,0:T(8,128)(2,1)S(1)} collective-permute-done((bf16[32,256]{1,0:T(8,128)(2,1)S(1)}, bf16[32,256]{1,0:T(8,128)(2,1)S(1)}, u32[]{:S(2)}, u32[]{:S(2)}) %collective-permute-start.20) | collective-permute-done | bytes 16416 | tf_op jit(solution)/shard_map/ppermute | solution.py:16
  132.1 1.9 collective-permute-start.23
  134.0 3.6 %collective-permute-start.22 = (bf16[32,256]{1,0:T(8,128)(2,1)S(1)}, bf16[32,256]{1,0:T(8,128)(2,1)S(1)}, u32[]{:S(2)}, u32[]{:S(2)}) collective-permute-start(bf16[32,256]{1,0:T(8,128)(2,1)S(1)} %get-tuple-element.14), channel_id=1, source_target_pairs={{0,1},{1,2},{2,3},{3,4},{4,5},{5,6},{6,7},{7,8},{8,9},{9,10},{10,1... | collective-permute-start | bytes 49160 | tf_op jit(solution)/shard_map/ppermute | solution.py:16
  137.6 3.0 %collective-permute-done.22 = bf16[32,256]{1,0:T(8,128)(2,1)S(1)} collective-permute-done((bf16[32,256]{1,0:T(8,128)(2,1)S(1)}, bf16[32,256]{1,0:T(8,128)(2,1)S(1)}, u32[]{:S(2)}, u32[]{:S(2)}) %collective-permute-start.22) | collective-permute-done | bytes 16416 | tf_op jit(solution)/shard_map/ppermute | solution.py:16
  142.8 1.9 collective-permute-start.25
  144.7 3.4 %collective-permute-start.24 = (bf16[32,256]{1,0:T(8,128)(2,1)S(1)}, bf16[32,256]{1,0:T(8,128)(2,1)S(1)}, u32[]{:S(2)}, u32[]{:S(2)}) collective-permute-start(bf16[32,256]{1,0:T(8,128)(2,1)S(1)} %get-tuple-element.12), channel_id=1, source_target_pairs={{0,1},{1,2},{2,3},{3,4},{4,5},{5,6},{6,7},{7,8},{8,9},{9,10},{10,1... | collective-permute-start | bytes 49160 | tf_op jit(solution)/shard_map/ppermute | solution.py:16
  148.1 3.2 %collective-permute-done.24 = bf16[32,256]{1,0:T(8,128)(2,1)S(1)} collective-permute-done((bf16[32,256]{1,0:T(8,128)(2,1)S(1)}, bf16[32,256]{1,0:T(8,128)(2,1)S(1)}, u32[]{:S(2)}, u32[]{:S(2)}) %collective-permute-start.24) | collective-permute-done | bytes 16416 | tf_op jit(solution)/shard_map/ppermute | solution.py:16
  155.0 3.4 %collective-permute-start.26 = (bf16[32,256]{1,0:T(8,128)(2,1)S(1)}, bf16[32,256]{1,0:T(8,128)(2,1)S(1)}, u32[]{:S(2)}, u32[]{:S(2)}) collective-permute-start(bf16[32,256]{1,0:T(8,128)(2,1)S(1)} %get-tuple-element.10), channel_id=1, source_target_pairs={{0,1},{1,2},{2,3},{3,4},{4,5},{5,6},{6,7},{7,8},{8,9},{9,10},{10,1... | collective-permute-start | bytes 49160 | tf_op jit(solution)/shard_map/ppermute | solution.py:16
  158.4 6.2 %gather_fusion = s32[1024]{0:T(1024)S(1)} fusion(s32[2048]{0:T(1024)S(1)} %bitcast.37, s32[1024]{0:T(1024)S(1)} %fusion.307), kind=kCustom, calls=%fused_computation | custom fusion | bytes 12288 | tf_op jit(solution)/shard_map/jit(_take)/gather | solution.py:103
  166.9 4.0 %collective-permute-start.29 = (bf16[32,256]{1,0:T(8,128)(2,1)S(1)}, bf16[32,256]{1,0:T(8,128)(2,1)S(1)}, u32[]{:S(2)}, u32[]{:S(2)}) collective-permute-start(bf16[32,256]{1,0:T(8,128)(2,1)S(1)} %get-tuple-element.9), channel_id=1, source_target_pairs={{1,0},{2,1},{3,2},{4,3},{5,4},{6,5},{7,6},{8,7},{9,8},{10,9},{11,1... | collective-permute-start | bytes 49160 | tf_op jit(solution)/shard_map/ppermute | solution.py:17
  170.9 1.9 collective-permute-start.28
  172.9 4.6 %collective-permute-done.28 = bf16[32,256]{1,0:T(8,128)(2,1)S(1)} collective-permute-done((bf16[32,256]{1,0:T(8,128)(2,1)S(1)}, bf16[32,256]{1,0:T(8,128)(2,1)S(1)}, u32[]{:S(2)}, u32[]{:S(2)}) %collective-permute-start.28) | collective-permute-done | bytes 16416 | tf_op jit(solution)/shard_map/ppermute | solution.py:16
  181.2 3.6 %collective-permute-start.30 = (bf16[32,256]{1,0:T(8,128)(2,1)S(1)}, bf16[32,256]{1,0:T(8,128)(2,1)S(1)}, u32[]{:S(2)}, u32[]{:S(2)}) collective-permute-start(bf16[32,256]{1,0:T(8,128)(2,1)S(1)} %get-tuple-element.6), channel_id=1, source_target_pairs={{0,1},{1,2},{2,3},{3,4},{4,5},{5,6},{6,7},{7,8},{8,9},{9,10},{10,1... | collective-permute-start | bytes 49160 | tf_op jit(solution)/shard_map/ppermute | solution.py:16
  184.9 2.9 %collective-permute-done.30 = bf16[32,256]{1,0:T(8,128)(2,1)S(1)} collective-permute-done((bf16[32,256]{1,0:T(8,128)(2,1)S(1)}, bf16[32,256]{1,0:T(8,128)(2,1)S(1)}, u32[]{:S(2)}, u32[]{:S(2)}) %collective-permute-start.30) | collective-permute-done | bytes 16416 | tf_op jit(solution)/shard_map/ppermute | solution.py:16
  190.5 10.0 %scatter_custom_fusion = f32[2048,128]{1,0:T(8,128)S(1)} fusion(s32[1024]{0:T(1024)S(1)} %get-tuple-element.48, f32[]{:T(128)} %constant.21.clone.1, pred[1024]{0:T(1024)(128)(4,1)S(1)} %compare_and_fusion, bf16[]{:T(256)} %constant.39.clone.1, bf16[32,128]{1,0:T(8,128)(2,1)S(1)} %bitcast_reduce_fusion, s32[1024]{0:T(1024)S(1)} %get-tuple-element.49), kind=kCustom, calls=%fused_computation.251 | custom fusion | flops 393216 | bytes 1061894 | tf_op jit(solution)/shard_map/scatter-add | solution.py:106
  201.4 45.0 %reduce-scatter.2.cloned.1.call-done = bf16[256,128]{1,0:T(8,128)(2,1)} async-done(((bf16[2048,128]{1,0:T(8,128)(2,1)}), bf16[256,128]{1,0:T(8,128)(2,1)}) %reduce-scatter.2.cloned.1.call-update) | async-done | bytes 65552 | tf_op jit(solution)/shard_map/reduce_scatter | solution.py:107
  (136 shorter events, 41.9 us)
Async XLA Ops:
  7.2 28.9 %copy-start = (bf16[3,256,256]{2,1,0:T(8,128)(2,1)S(1)}, bf16[3,256,256]{2,1,0:T(8,128)(2,1)}, u32[]{:S(2)}) copy-start(bf16[3,256,256]{2,1,0:T(8,128)(2,1)} %param.19) | copy-start | bytes 1179652
  7.2 16.7 %copy-start.2 = (bf16[512,128]{1,0:T(8,128)(2,1)S(1)}, bf16[512,128]{1,0:T(8,128)(2,1)}, u32[]{:S(2)}) copy-start(bf16[512,128]{1,0:T(8,128)(2,1)} %param.15) | copy-start | bytes 393220
  7.2 12.0 %copy-start.4 = (f32[512,4]{0,1:T(4,128)S(1)}, f32[512,4]{0,1:T(4,128)}, u32[]{:S(2)}) copy-start(f32[512,4]{0,1:T(4,128)} %param.17) | copy-start | bytes 24580
  7.2 12.1 %copy-start.7 = (s32[512,4]{0,1:T(4,128)S(1)}, s32[512,4]{0,1:T(4,128)}, u32[]{:S(2)}) copy-start(s32[512,4]{0,1:T(4,128)} %param.16) | copy-start | bytes 24580
  7.2 239.2 %reduce-scatter.2.cloned.1.call-start = ((), (), s32[]{:S(2)}) async-start(), calls=%async_computation.1 | async-start | bytes 589824 | tf_op jit(solution)/shard_map/reduce_scatter | solution.py:107
  9.6 9.7 %collective-permute-start.1 = (bf16[32,256]{1,0:T(8,128)(2,1)S(1)}, bf16[32,256]{1,0:T(8,128)(2,1)S(1)}, u32[]{:S(2)}, u32[]{:S(2)}) collective-permute-start(bf16[32,256]{1,0:T(8,128)(2,1)S(1)} %get-tuple-element.37), channel_id=1, source_target_pairs={{1,0},{2,1},{3,2},{4,3},{5,4},{6,5},{7,6},{8,7},{9,8},{10,9},{11,1... | collective-permute-start | bytes 49160 | tf_op jit(solution)/shard_map/ppermute | solution.py:17
  17.3 6.6 %collective-permute-start = (bf16[32,256]{1,0:T(8,128)(2,1)S(1)}, bf16[32,256]{1,0:T(8,128)(2,1)S(1)}, u32[]{:S(2)}, u32[]{:S(2)}) collective-permute-start(bf16[32,256]{1,0:T(8,128)(2,1)S(1)} %get-tuple-element.36), channel_id=1, source_target_pairs={{0,1},{1,2},{2,3},{3,4},{4,5},{5,6},{6,7},{7,8},{8,9},{9,10},{10,1... | collective-permute-start | bytes 49160 | tf_op jit(solution)/shard_map/ppermute | solution.py:16
  25.1 0.7 copy-start.3
  26.0 5.3 %collective-permute-start.3 = (bf16[32,256]{1,0:T(8,128)(2,1)S(1)}, bf16[32,256]{1,0:T(8,128)(2,1)S(1)}, u32[]{:S(2)}, u32[]{:S(2)}) collective-permute-start(bf16[32,256]{1,0:T(8,128)(2,1)S(1)} %get-tuple-element.35), channel_id=1, source_target_pairs={{1,0},{2,1},{3,2},{4,3},{5,4},{6,5},{7,6},{8,7},{9,8},{10,9},{11,1... | collective-permute-start | bytes 49160 | tf_op jit(solution)/shard_map/ppermute | solution.py:17
  27.9 6.6 %collective-permute-start.2 = (bf16[32,256]{1,0:T(8,128)(2,1)S(1)}, bf16[32,256]{1,0:T(8,128)(2,1)S(1)}, u32[]{:S(2)}, u32[]{:S(2)}) collective-permute-start(bf16[32,256]{1,0:T(8,128)(2,1)S(1)} %get-tuple-element.34), channel_id=1, source_target_pairs={{0,1},{1,2},{2,3},{3,4},{4,5},{5,6},{6,7},{7,8},{8,9},{9,10},{10,1... | collective-permute-start | bytes 49160 | tf_op jit(solution)/shard_map/ppermute | solution.py:16
  35.7 0.7 copy-start.10
  37.1 5.3 %collective-permute-start.5 = (bf16[32,256]{1,0:T(8,128)(2,1)S(1)}, bf16[32,256]{1,0:T(8,128)(2,1)S(1)}, u32[]{:S(2)}, u32[]{:S(2)}) collective-permute-start(bf16[32,256]{1,0:T(8,128)(2,1)S(1)} %get-tuple-element.33), channel_id=1, source_target_pairs={{1,0},{2,1},{3,2},{4,3},{5,4},{6,5},{7,6},{8,7},{9,8},{10,9},{11,1... | collective-permute-start | bytes 49160 | tf_op jit(solution)/shard_map/ppermute | solution.py:17
  39.0 6.6 %collective-permute-start.4 = (bf16[32,256]{1,0:T(8,128)(2,1)S(1)}, bf16[32,256]{1,0:T(8,128)(2,1)S(1)}, u32[]{:S(2)}, u32[]{:S(2)}) collective-permute-start(bf16[32,256]{1,0:T(8,128)(2,1)S(1)} %get-tuple-element.32), channel_id=1, source_target_pairs={{0,1},{1,2},{2,3},{3,4},{4,5},{5,6},{6,7},{7,8},{8,9},{9,10},{10,1... | collective-permute-start | bytes 49160 | tf_op jit(solution)/shard_map/ppermute | solution.py:16
  47.4 5.3 %collective-permute-start.7 = (bf16[32,256]{1,0:T(8,128)(2,1)S(1)}, bf16[32,256]{1,0:T(8,128)(2,1)S(1)}, u32[]{:S(2)}, u32[]{:S(2)}) collective-permute-start(bf16[32,256]{1,0:T(8,128)(2,1)S(1)} %get-tuple-element.31), channel_id=1, source_target_pairs={{1,0},{2,1},{3,2},{4,3},{5,4},{6,5},{7,6},{8,7},{9,8},{10,9},{11,1... | collective-permute-start | bytes 49160 | tf_op jit(solution)/shard_map/ppermute | solution.py:17
  49.3 6.6 %collective-permute-start.6 = (bf16[32,256]{1,0:T(8,128)(2,1)S(1)}, bf16[32,256]{1,0:T(8,128)(2,1)S(1)}, u32[]{:S(2)}, u32[]{:S(2)}) collective-permute-start(bf16[32,256]{1,0:T(8,128)(2,1)S(1)} %get-tuple-element.30), channel_id=1, source_target_pairs={{0,1},{1,2},{2,3},{3,4},{4,5},{5,6},{6,7},{7,8},{8,9},{9,10},{10,1... | collective-permute-start | bytes 49160 | tf_op jit(solution)/shard_map/ppermute | solution.py:16
  57.1 0.9 copy-start.8
  57.1 0.9 copy-start.11
  58.6 5.3 %collective-permute-start.9 = (bf16[32,256]{1,0:T(8,128)(2,1)S(1)}, bf16[32,256]{1,0:T(8,128)(2,1)S(1)}, u32[]{:S(2)}, u32[]{:S(2)}) collective-permute-start(bf16[32,256]{1,0:T(8,128)(2,1)S(1)} %get-tuple-element.29), channel_id=1, source_target_pairs={{1,0},{2,1},{3,2},{4,3},{5,4},{6,5},{7,6},{8,7},{9,8},{10,9},{11,1... | collective-permute-start | bytes 49160 | tf_op jit(solution)/shard_map/ppermute | solution.py:17
  60.6 6.6 %collective-permute-start.8 = (bf16[32,256]{1,0:T(8,128)(2,1)S(1)}, bf16[32,256]{1,0:T(8,128)(2,1)S(1)}, u32[]{:S(2)}, u32[]{:S(2)}) collective-permute-start(bf16[32,256]{1,0:T(8,128)(2,1)S(1)} %get-tuple-element.28), channel_id=1, source_target_pairs={{0,1},{1,2},{2,3},{3,4},{4,5},{5,6},{6,7},{7,8},{8,9},{9,10},{10,1... | collective-permute-start | bytes 49160 | tf_op jit(solution)/shard_map/ppermute | solution.py:16
  68.9 5.5 %collective-permute-start.11 = (bf16[32,256]{1,0:T(8,128)(2,1)S(1)}, bf16[32,256]{1,0:T(8,128)(2,1)S(1)}, u32[]{:S(2)}, u32[]{:S(2)}) collective-permute-start(bf16[32,256]{1,0:T(8,128)(2,1)S(1)} %get-tuple-element.27), channel_id=1, source_target_pairs={{1,0},{2,1},{3,2},{4,3},{5,4},{6,5},{7,6},{8,7},{9,8},{10,9},{11,1... | collective-permute-start | bytes 49160 | tf_op jit(solution)/shard_map/ppermute | solution.py:17
  70.9 6.6 %collective-permute-start.10 = (bf16[32,256]{1,0:T(8,128)(2,1)S(1)}, bf16[32,256]{1,0:T(8,128)(2,1)S(1)}, u32[]{:S(2)}, u32[]{:S(2)}) collective-permute-start(bf16[32,256]{1,0:T(8,128)(2,1)S(1)} %get-tuple-element.26), channel_id=1, source_target_pairs={{0,1},{1,2},{2,3},{3,4},{4,5},{5,6},{6,7},{7,8},{8,9},{9,10},{10,1... | collective-permute-start | bytes 49160 | tf_op jit(solution)/shard_map/ppermute | solution.py:16
  79.7 5.3 %collective-permute-start.13 = (bf16[32,256]{1,0:T(8,128)(2,1)S(1)}, bf16[32,256]{1,0:T(8,128)(2,1)S(1)}, u32[]{:S(2)}, u32[]{:S(2)}) collective-permute-start(bf16[32,256]{1,0:T(8,128)(2,1)S(1)} %get-tuple-element.25), channel_id=1, source_target_pairs={{1,0},{2,1},{3,2},{4,3},{5,4},{6,5},{7,6},{8,7},{9,8},{10,9},{11,1... | collective-permute-start | bytes 49160 | tf_op jit(solution)/shard_map/ppermute | solution.py:17
  81.6 6.6 %collective-permute-start.12 = (bf16[32,256]{1,0:T(8,128)(2,1)S(1)}, bf16[32,256]{1,0:T(8,128)(2,1)S(1)}, u32[]{:S(2)}, u32[]{:S(2)}) collective-permute-start(bf16[32,256]{1,0:T(8,128)(2,1)S(1)} %get-tuple-element.24), channel_id=1, source_target_pairs={{0,1},{1,2},{2,3},{3,4},{4,5},{5,6},{6,7},{7,8},{8,9},{9,10},{10,1... | collective-permute-start | bytes 49160 | tf_op jit(solution)/shard_map/ppermute | solution.py:16
  90.0 5.3 %collective-permute-start.15 = (bf16[32,256]{1,0:T(8,128)(2,1)S(1)}, bf16[32,256]{1,0:T(8,128)(2,1)S(1)}, u32[]{:S(2)}, u32[]{:S(2)}) collective-permute-start(bf16[32,256]{1,0:T(8,128)(2,1)S(1)} %get-tuple-element.23), channel_id=1, source_target_pairs={{1,0},{2,1},{3,2},{4,3},{5,4},{6,5},{7,6},{8,7},{9,8},{10,9},{11,1... | collective-permute-start | bytes 49160 | tf_op jit(solution)/shard_map/ppermute | solution.py:17
  91.9 6.6 %collective-permute-start.14 = (bf16[32,256]{1,0:T(8,128)(2,1)S(1)}, bf16[32,256]{1,0:T(8,128)(2,1)S(1)}, u32[]{:S(2)}, u32[]{:S(2)}) collective-permute-start(bf16[32,256]{1,0:T(8,128)(2,1)S(1)} %get-tuple-element.22), channel_id=1, source_target_pairs={{0,1},{1,2},{2,3},{3,4},{4,5},{5,6},{6,7},{7,8},{8,9},{9,10},{10,1... | collective-permute-start | bytes 49160 | tf_op jit(solution)/shard_map/ppermute | solution.py:16
  100.7 5.3 %collective-permute-start.17 = (bf16[32,256]{1,0:T(8,128)(2,1)S(1)}, bf16[32,256]{1,0:T(8,128)(2,1)S(1)}, u32[]{:S(2)}, u32[]{:S(2)}) collective-permute-start(bf16[32,256]{1,0:T(8,128)(2,1)S(1)} %get-tuple-element.21), channel_id=1, source_target_pairs={{1,0},{2,1},{3,2},{4,3},{5,4},{6,5},{7,6},{8,7},{9,8},{10,9},{11,1... | collective-permute-start | bytes 49160 | tf_op jit(solution)/shard_map/ppermute | solution.py:17
  102.6 6.6 %collective-permute-start.16 = (bf16[32,256]{1,0:T(8,128)(2,1)S(1)}, bf16[32,256]{1,0:T(8,128)(2,1)S(1)}, u32[]{:S(2)}, u32[]{:S(2)}) collective-permute-start(bf16[32,256]{1,0:T(8,128)(2,1)S(1)} %get-tuple-element.20), channel_id=1, source_target_pairs={{0,1},{1,2},{2,3},{3,4},{4,5},{5,6},{6,7},{7,8},{8,9},{9,10},{10,1... | collective-permute-start | bytes 49160 | tf_op jit(solution)/shard_map/ppermute | solution.py:16
  111.0 5.3 %collective-permute-start.19 = (bf16[32,256]{1,0:T(8,128)(2,1)S(1)}, bf16[32,256]{1,0:T(8,128)(2,1)S(1)}, u32[]{:S(2)}, u32[]{:S(2)}) collective-permute-start(bf16[32,256]{1,0:T(8,128)(2,1)S(1)} %get-tuple-element.19), channel_id=1, source_target_pairs={{1,0},{2,1},{3,2},{4,3},{5,4},{6,5},{7,6},{8,7},{9,8},{10,9},{11,1... | collective-permute-start | bytes 49160 | tf_op jit(solution)/shard_map/ppermute | solution.py:17
  112.9 6.6 %collective-permute-start.18 = (bf16[32,256]{1,0:T(8,128)(2,1)S(1)}, bf16[32,256]{1,0:T(8,128)(2,1)S(1)}, u32[]{:S(2)}, u32[]{:S(2)}) collective-permute-start(bf16[32,256]{1,0:T(8,128)(2,1)S(1)} %get-tuple-element.18), channel_id=1, source_target_pairs={{0,1},{1,2},{2,3},{3,4},{4,5},{5,6},{6,7},{7,8},{8,9},{9,10},{10,1... | collective-permute-start | bytes 49160 | tf_op jit(solution)/shard_map/ppermute | solution.py:16
  121.8 5.3 %collective-permute-start.21 = (bf16[32,256]{1,0:T(8,128)(2,1)S(1)}, bf16[32,256]{1,0:T(8,128)(2,1)S(1)}, u32[]{:S(2)}, u32[]{:S(2)}) collective-permute-start(bf16[32,256]{1,0:T(8,128)(2,1)S(1)} %get-tuple-element.17), channel_id=1, source_target_pairs={{1,0},{2,1},{3,2},{4,3},{5,4},{6,5},{7,6},{8,7},{9,8},{10,9},{11,1... | collective-permute-start | bytes 49160 | tf_op jit(solution)/shard_map/ppermute | solution.py:17
  123.7 6.6 %collective-permute-start.20 = (bf16[32,256]{1,0:T(8,128)(2,1)S(1)}, bf16[32,256]{1,0:T(8,128)(2,1)S(1)}, u32[]{:S(2)}, u32[]{:S(2)}) collective-permute-start(bf16[32,256]{1,0:T(8,128)(2,1)S(1)} %get-tuple-element.16), channel_id=1, source_target_pairs={{0,1},{1,2},{2,3},{3,4},{4,5},{5,6},{6,7},{7,8},{8,9},{9,10},{10,1... | collective-permute-start | bytes 49160 | tf_op jit(solution)/shard_map/ppermute | solution.py:16
  132.1 5.5 %collective-permute-start.23 = (bf16[32,256]{1,0:T(8,128)(2,1)S(1)}, bf16[32,256]{1,0:T(8,128)(2,1)S(1)}, u32[]{:S(2)}, u32[]{:S(2)}) collective-permute-start(bf16[32,256]{1,0:T(8,128)(2,1)S(1)} %get-tuple-element.15), channel_id=1, source_target_pairs={{1,0},{2,1},{3,2},{4,3},{5,4},{6,5},{7,6},{8,7},{9,8},{10,9},{11,1... | collective-permute-start | bytes 49160 | tf_op jit(solution)/shard_map/ppermute | solution.py:17
  134.0 6.6 %collective-permute-start.22 = (bf16[32,256]{1,0:T(8,128)(2,1)S(1)}, bf16[32,256]{1,0:T(8,128)(2,1)S(1)}, u32[]{:S(2)}, u32[]{:S(2)}) collective-permute-start(bf16[32,256]{1,0:T(8,128)(2,1)S(1)} %get-tuple-element.14), channel_id=1, source_target_pairs={{0,1},{1,2},{2,3},{3,4},{4,5},{5,6},{6,7},{7,8},{8,9},{9,10},{10,1... | collective-permute-start | bytes 49160 | tf_op jit(solution)/shard_map/ppermute | solution.py:16
  142.8 5.3 %collective-permute-start.25 = (bf16[32,256]{1,0:T(8,128)(2,1)S(1)}, bf16[32,256]{1,0:T(8,128)(2,1)S(1)}, u32[]{:S(2)}, u32[]{:S(2)}) collective-permute-start(bf16[32,256]{1,0:T(8,128)(2,1)S(1)} %get-tuple-element.13), channel_id=1, source_target_pairs={{1,0},{2,1},{3,2},{4,3},{5,4},{6,5},{7,6},{8,7},{9,8},{10,9},{11,1... | collective-permute-start | bytes 49160 | tf_op jit(solution)/shard_map/ppermute | solution.py:17
  144.7 6.6 %collective-permute-start.24 = (bf16[32,256]{1,0:T(8,128)(2,1)S(1)}, bf16[32,256]{1,0:T(8,128)(2,1)S(1)}, u32[]{:S(2)}, u32[]{:S(2)}) collective-permute-start(bf16[32,256]{1,0:T(8,128)(2,1)S(1)} %get-tuple-element.12), channel_id=1, source_target_pairs={{0,1},{1,2},{2,3},{3,4},{4,5},{5,6},{6,7},{7,8},{8,9},{9,10},{10,1... | collective-permute-start | bytes 49160 | tf_op jit(solution)/shard_map/ppermute | solution.py:16
  152.5 5.9 %copy-start.6 = (s32[1024]{0:T(1024)S(1)}, s32[1024]{0:T(1024)}, u32[]{:S(2)}) copy-start(s32[1024]{0:T(1024)} %param.26) | copy-start | bytes 12292
  152.5 5.9 %copy-start.1 = (s32[1,2048]{1,0:T(1,128)S(1)}, s32[1,2048]{1,0:T(1,128)}, u32[]{:S(2)}) copy-start(s32[1,2048]{1,0:T(1,128)} %param.27) | copy-start | bytes 24580
  153.1 11.5 %collective-permute-start.27 = (bf16[32,256]{1,0:T(8,128)(2,1)S(1)}, bf16[32,256]{1,0:T(8,128)(2,1)S(1)}, u32[]{:S(2)}, u32[]{:S(2)}) collective-permute-start(bf16[32,256]{1,0:T(8,128)(2,1)S(1)} %get-tuple-element.11), channel_id=1, source_target_pairs={{1,0},{2,1},{3,2},{4,3},{5,4},{6,5},{7,6},{8,7},{9,8},{10,9},{11,1... | collective-permute-start | bytes 49160 | tf_op jit(solution)/shard_map/ppermute | solution.py:17
  155.0 9.6 %collective-permute-start.26 = (bf16[32,256]{1,0:T(8,128)(2,1)S(1)}, bf16[32,256]{1,0:T(8,128)(2,1)S(1)}, u32[]{:S(2)}, u32[]{:S(2)}) collective-permute-start(bf16[32,256]{1,0:T(8,128)(2,1)S(1)} %get-tuple-element.10), channel_id=1, source_target_pairs={{0,1},{1,2},{2,3},{3,4},{4,5},{5,6},{6,7},{7,8},{8,9},{9,10},{10,1... | collective-permute-start | bytes 49160 | tf_op jit(solution)/shard_map/ppermute | solution.py:16
  166.2 6.7 %copy-start.5 = (s32[1024]{0:T(1024)S(1)}, s32[1024]{0:T(1024)}, u32[]{:S(2)}) copy-start(s32[1024]{0:T(1024)} %param.25) | copy-start | bytes 12292
  166.9 6.0 %collective-permute-start.29 = (bf16[32,256]{1,0:T(8,128)(2,1)S(1)}, bf16[32,256]{1,0:T(8,128)(2,1)S(1)}, u32[]{:S(2)}, u32[]{:S(2)}) collective-permute-start(bf16[32,256]{1,0:T(8,128)(2,1)S(1)} %get-tuple-element.9), channel_id=1, source_target_pairs={{1,0},{2,1},{3,2},{4,3},{5,4},{6,5},{7,6},{8,7},{9,8},{10,9},{11,1... | collective-permute-start | bytes 49160 | tf_op jit(solution)/shard_map/ppermute | solution.py:17
  170.9 6.6 %collective-permute-start.28 = (bf16[32,256]{1,0:T(8,128)(2,1)S(1)}, bf16[32,256]{1,0:T(8,128)(2,1)S(1)}, u32[]{:S(2)}, u32[]{:S(2)}) collective-permute-start(bf16[32,256]{1,0:T(8,128)(2,1)S(1)} %get-tuple-element.8), channel_id=1, source_target_pairs={{0,1},{1,2},{2,3},{3,4},{4,5},{5,6},{6,7},{7,8},{8,9},{9,10},{10,1... | collective-permute-start | bytes 49160 | tf_op jit(solution)/shard_map/ppermute | solution.py:16
  179.3 5.6 %collective-permute-start.31 = (bf16[32,256]{1,0:T(8,128)(2,1)S(1)}, bf16[32,256]{1,0:T(8,128)(2,1)S(1)}, u32[]{:S(2)}, u32[]{:S(2)}) collective-permute-start(bf16[32,256]{1,0:T(8,128)(2,1)S(1)} %get-tuple-element.7), channel_id=1, source_target_pairs={{1,0},{2,1},{3,2},{4,3},{5,4},{6,5},{7,6},{8,7},{9,8},{10,9},{11,1... | collective-permute-start | bytes 49160 | tf_op jit(solution)/shard_map/ppermute | solution.py:17
  181.2 6.6 %collective-permute-start.30 = (bf16[32,256]{1,0:T(8,128)(2,1)S(1)}, bf16[32,256]{1,0:T(8,128)(2,1)S(1)}, u32[]{:S(2)}, u32[]{:S(2)}) collective-permute-start(bf16[32,256]{1,0:T(8,128)(2,1)S(1)} %get-tuple-element.6), channel_id=1, source_target_pairs={{0,1},{1,2},{2,3},{3,4},{4,5},{5,6},{6,7},{7,8},{8,9},{9,10},{10,1... | collective-permute-start | bytes 49160 | tf_op jit(solution)/shard_map/ppermute | solution.py:16
  189.4 0.8 copy-start.9
  189.4 0.8 copy-start.12
  190.1 11.2 %copy-start.13 = (bf16[512,128]{1,0:T(8,128)(2,1)}, bf16[512,128]{1,0:T(8,128)(2,1)S(1)}, u32[]{:S(2)}) copy-start(bf16[512,128]{1,0:T(8,128)(2,1)S(1)} %fusion.44) | copy-start | bytes 393220
Sparse Core Ops, SparseCore 0:
  201.5 44.8 reduce-scatter.1
where the time goes:
time: 259 us; the launch traced here: 255 us
  waiting for transfers between devices  95.4 us (37%)
  starting transfers between devices  90.2 us (35%)
  matrix products  26.9 us (10%)
  other arithmetic  18.2 us (7%)
  between operations  15 us (6%)
  local copies, waits for them, and re-layouts  9.03 us (3%)
    ppermute x16, starting transfers between devices, extended_2(): before = lax.ppermute(last, axis, up)  51.6 us
    ppermute x16, waiting for transfers between devices, extended_2(): before = lax.ppermute(last, axis, up)  50.3 us
    reduce_scatter x1, waiting for transfers between devices, per_device(): lax.psum_scatter(partial_paths.astype(jnp.bfloat16), 'region', scatter_di...  45 us
    ppermute x16, starting transfers between devices, extended_2(): after = lax.ppermute(leading, axis, down)  38.6 us
    dot_general x16, matrix products, spread(): jnp.dot(picker_rows, table, preferred_element_type=jnp.float32)  19.3 us
    scatter-add x1, other arithmetic, per_device(): partial_paths = jax.ops.segment_sum(vals, slots, num_segments=paths_col)  9.98 us
    gather x1, local copies, waits for them, and re-layouts, per_device(): slots = jnp.take(path_slot[0], inc_path)  6.15 us
    convert_element_type x16, other arithmetic, spread(): return acc.astype(jnp.bfloat16)  5.45 us
  transfers between devices with their start and end apart: 33, of which 16 were waited for; matrix products, arithmetic and copies ran while one was open for 2% of the time, Pallas kernels for 0%

commit v1 on v0

v1 whole, which is shorter than its diff:
```python
import functools

import jax
import jax.numpy as jnp
from jax import lax
from jax.experimental import pallas as pl
from jax.experimental.pallas import tpu as pltpu
from jax.sharding import PartitionSpec as P

MESH = pl.DeviceIdType.MESH
SEG, WIDTH, BND, NBLK, BS = 512, 128, 32, 32, 16
LAGS, ENT, PATHS = 4, 1024, 2048
SLOT_HI = PATHS // WIDTH
F32, BF16 = jnp.float32, jnp.bfloat16


def dot(a, b):
    return jnp.dot(a, b, preferred_element_type=F32)


def iota(shape, dim):
    return lax.broadcasted_iota(jnp.int32, shape, dim)


def sigmoid(v):
    return 0.5 * jnp.tanh(0.5 * v) + 0.5


def kernel(
    nr, nd,
    nbr_h, ew_h, bnd_h, h0_h, x_h, wg_h, wc_h, wo_h, bg_h, bc_h, bo_h, ib_h, ip_h, ps_h,
    sf_o, pt_o,
    nbr, ew, bnd, x, wx, wgh, wch, wo, bg, bc, bo, ib, ip, ps,
    h, hb, rhb, m, ar, pk, s, aa, g, acc, s12, sx, gx, pre, upd,
    e0, r0, ex, rx, eh, rh,
    cnt, crecv, ct, btsend, btrecv, ptv,
    load_sem, send_sem, recv_sem, c_send, c_recv, b_send, b_recv, out_sem,
):
    region, dom = lax.axis_index("region"), lax.axis_index("dom")
    up1, dn1 = lax.rem(dom + 1, nd), lax.rem(dom + nd - 1, nd)
    up2, dn2 = lax.rem(dom + 2, nd), lax.rem(dom + nd - 2, nd)
    peers = [None] + [lax.rem(region + k, nr) for k in range(1, nr)]
    own_hi = SLOT_HI // nr
    own_rows = own_hi * NBLK

    loads = []

    def load(src, dst):
        copy = pltpu.make_async_copy(src, dst, load_sem.at[len(loads)])
        copy.start()
        loads.append(copy)
        return copy

    l_graph = [load(nbr_h, nbr), load(ew_h, ew), load(bnd_h, bnd)]
    l_h0 = load(h0_h, hb)
    l_x = load(x_h, x)
    l_path = [load(ib_h, ib), load(ip_h, ip), load(ps_h, ps)]
    l_w = [
        load(wg_h.at[:, 0:WIDTH, :], wx.at[:, :, 0 : 2 * WIDTH]),
        load(wc_h.at[:, 0:WIDTH, :], wx.at[:, :, 2 * WIDTH : 3 * WIDTH]),
        load(wg_h.at[:, WIDTH : 2 * WIDTH, :], wgh),
        load(wc_h.at[:, WIDTH : 2 * WIDTH, :], wch),
        load(bg_h, bg),
        load(bc_h, bc),
        load(wo_h, wo),
        load(bo_h, bo),
    ]

    barrier = pltpu.get_barrier_semaphore()
    for there in (up1, dn1, up2, dn2):
        pl.semaphore_signal(barrier, inc=1, device_id={"dom": there}, device_id_type=MESH)
    for k in range(1, nr):
        pl.semaphore_signal(barrier, inc=1, device_id={"region": peers[k]}, device_id_type=MESH)

    for c in l_graph:
        c.wait()
    near = nbr[...]
    outside = ((dom == 0) & (near >= SEG) & (near < SEG + BND)) | (
        (dom == nd - 1) & (near >= SEG + BND)
    )
    near = jnp.where(outside, -1, near).astype(F32)
    raw = ew[...]
    wts = raw / jnp.sum(raw, axis=0, keepdims=True)
    tall = jnp.transpose(jnp.concatenate([near, wts], axis=0))
    step = 32
    lanes = iota((step, SEG + WIDTH), 1).astype(F32)
    for i in range(0, SEG, step):
        a = jnp.zeros((step, SEG + WIDTH), F32)
        for k in range(4):
            a = a + jnp.where(lanes == tall[i : i + step, k : k + 1], tall[i : i + step, 4 + k : 5 + k], 0.0)
        a = a.astype(BF16)
        m[i : i + step, 0:SEG] = a[:, 0:SEG]
        ar[i : i + step, :] = a[:, SEG:]

    turn = lax.rem(iota((2 * BND, 2 * BND), 0) + BND, 2 * BND) == iota((2 * BND, 2 * BND), 1)
    picked = jnp.sum(jnp.where(turn, bnd[...].astype(F32), 0.0), axis=1, keepdims=True)
    picker = (iota((2 * BND, SEG), 1).astype(F32) == picked).astype(F32).astype(BF16)
    pk[0 : 2 * BND, :] = picker
    pk[2 * BND :, :] = jnp.zeros((2 * BND, SEG), BF16)
    a_bnd = dot(picker, m[0:SEG, 0:SEG]).astype(BF16)
    s[0:32, :] = picker[0:32]
    s[32:64, :] = a_bnd[0:32]
    s[64:96, :] = picker[32:64]
    s[96:128, :] = a_bnd[32:64]

    sends = []

    def exchange(n, src, dst, far):
        lo, hi = far
        plan = (
            (src.at[0:64], dst.at[0:64], up1),
            (src.at[64:128], dst.at[64:128], dn1),
            (src.at[0:32, lo:hi], dst.at[128:160, lo:hi], up2),
            (src.at[64:96, lo:hi], dst.at[160:192, lo:hi], dn2),
        )
        copies = []
        for j, (a, b, there) in enumerate(plan):
            copy = pltpu.make_async_remote_copy(
                src_ref=a, dst_ref=b, send_sem=send_sem.at[n, j], recv_sem=recv_sem.at[n, j],
                device_id={"dom": there}, device_id_type=MESH,
            )
            copy.start()
            copies.append(copy)
        sends.extend(copies)
        return copies

    l_h0.wait()
    e0[:, 0:WIDTH] = dot(s[...], hb[...]).astype(BF16)
    e0[:, WIDTH:] = dot(s[...], ar[...]).astype(BF16)
    pl.semaphore_wait(barrier, 4 + nr - 1)
    first = exchange(0, e0, r0, (0, WIDTH))
    l_x.wait()
    x_moves = []
    for pair in range(2):
        cols = slice(pair * 256, pair * 256 + 256)
        ex[pair] = dot(s[...], x[:, cols]).astype(BF16)
        x_moves.append(exchange(1 + pair, ex.at[pair], rx.at[pair], (0, 256)))

    r0[192:256, :] = jnp.zeros((64, 256), BF16)
    rx[:, 192:256, :] = jnp.zeros((2, 64, 256), BF16)
    rh[:, 192:256, :] = jnp.zeros((2 * LAGS - 1, 64, WIDTH), BF16)
    row, col = iota((WIDTH, 2 * WIDTH), 0), iota((WIDTH, 2 * WIDTH), 1)
    place = ((row < 32) & (col == row)) | ((row >= 32) & (row < 64) & (col == row + 32))
    m[0:SEG, SEG:] = dot(ar[...], place.astype(F32).astype(BF16)).astype(BF16)
    aa[...] = dot(m[0:SEG, 0:SEG], m[0:SEG, :])

    for c in l_path:
        c.wait()
    path = ip[...]
    path_hi, path_lo = lax.shift_right_logical(path, 7), path & (WIDTH - 1)
    which = (iota((SLOT_HI, ENT), 0) == path_hi).astype(F32).astype(BF16)
    slots = ps[...]
    slots_hi = lax.shift_right_logical(slots, 7).astype(F32).astype(BF16)
    slots_lo = (slots & (WIDTH - 1)).astype(F32).astype(BF16)
    at_lo = iota((WIDTH, ENT), 0) == path_lo
    contract0 = (((0,), (0,)), ((), ()))
    slot_hi = jnp.sum(
        jnp.where(at_lo, lax.dot_general(slots_hi, which, contract0, preferred_element_type=F32), 0.0),
        axis=0, keepdims=True,
    )
    slot_lo = jnp.sum(
        jnp.where(at_lo, lax.dot_general(slots_lo, which, contract0, preferred_element_type=F32), 0.0),
        axis=0, keepdims=True,
    )
    target = slot_hi * NBLK + ib[...].astype(F32)
    ones_lo = (iota((WIDTH, ENT), 0).astype(F32) == slot_lo).astype(F32).astype(BF16)
    for i in range(0, SLOT_HI * NBLK, 128):
        ones = (iota((128, ENT), 0).astype(F32) + float(i) == target).astype(F32).astype(BF16)
        count = lax.dot_general(ones, ones_lo, (((1,), (1,)), ((), ())), preferred_element_type=F32)
        top = count.astype(BF16)
        cnt[0, i : i + 128, :] = top
        cnt[1, i : i + 128, :] = (count - top.astype(F32)).astype(BF16)
    c_moves = []
    for k in range(1, nr):
        copy = pltpu.make_async_remote_copy(
            src_ref=cnt.at[:, pl.ds(pl.multiple_of(peers[k] * own_rows, own_rows), own_rows), :],
            dst_ref=crecv.at[k],
            send_sem=c_send.at[k], recv_sem=c_recv.at[k],
            device_id={"region": peers[k]}, device_id_type=MESH,
        )
        copy.start()
        c_moves.append(copy)
    crecv[0] = cnt[:, pl.ds(pl.multiple_of(region * own_rows, own_rows), own_rows), :]

    for c in first:
        c.wait_recv()
    lane = iota((32, WIDTH), 1)
    b_low, b_up = r0[0:32, WIDTH:].astype(F32), r0[64:96, WIDTH:].astype(F32)
    g_row, g_col = iota((32, WIDTH), 0), iota((32, WIDTH), 1)
    g[0:32, SEG : SEG + WIDTH] = (g_col == g_row + 32).astype(F32).astype(BF16)
    g[32:64, SEG : SEG + WIDTH] = (g_col == g_row + 96).astype(F32).astype(BF16)
    g[0:32, SEG + WIDTH :] = jnp.where(lane < 32, b_low, 0.0).astype(BF16)
    g[32:64, SEG + WIDTH :] = jnp.where((lane >= 32) & (lane < 64), b_up, 0.0).astype(BF16)
    back = jnp.concatenate(
        [jnp.where((lane >= 32) & (lane < 64), b_low, 0.0), jnp.where(lane < 32, b_up, 0.0)], axis=0
    ).astype(BF16)
    g[0:64, 0:SEG] = dot(back, pk[...]).astype(BF16)
    g[64:128, :] = jnp.zeros((64, SEG + 2 * WIDTH), BF16)
    m[SEG:, :] = (aa[...] + dot(ar[...], g[...])).astype(BF16)

    for c in l_w:
        c.wait()

    def x_spread(pair):
        cols = slice(pair * 256, pair * 256 + 256)
        for c in x_moves[pair]:
            c.wait_recv()
        sx[pair] = (dot(m[:, 0:SEG], x[:, cols]) + dot(m[:, SEG:], rx[pair])).astype(BF16)

    def x_project(t):
        pair, cols = t // 2, slice((t % 2) * WIDTH, (t % 2 + 1) * WIDTH)
        bias = jnp.concatenate([bg[...], bc[...]], axis=1)
        gx[t] = (
            dot(x[:, t * WIDTH : (t + 1) * WIDTH], wx[0])
            + dot(sx[pair, 0:SEG, cols], wx[1])
            + dot(sx[pair, SEG:, cols], wx[2])
            + bias
        )

    def arrive(field, recv):
        both = acc[...] + dot(m[:, SEG:], recv)
        s12[:, 0:WIDTH] = both[0:SEG].astype(BF16)
        s12[:, WIDTH:] = both[SEG:].astype(BF16)

    def send_field(n, field):
        eh[n] = dot(s[...], field).astype(BF16)
        return exchange(3 + n, eh.at[n], rh.at[n], (0, WIDTH))

    h[...] = hb[...].astype(F32)
    x_spread(0)
    x_project(0)
    moving = None
    for t in range(LAGS):
        acc[...] = dot(m[:, 0:SEG], hb[...])
        pre[...] = gx[t, :, 0 : 2 * WIDTH] + dot(hb[...], wgh[0])
        if t == 1:
            x_project(2)
        if t == 2:
            x_project(3)
        if t == 0:
            arrive(hb, r0[:, 0:WIDTH])
        else:
            for c in moving:
                c.wait_recv()
            arrive(hb, rh[2 * t - 1])
        w12 = wgh[1:3].reshape(2 * WIDTH, 2 * WIDTH)
        reset = sigmoid(pre[:, 0:WIDTH] + dot(s12[...], w12[:, 0:WIDTH]))
        rhb[...] = (reset * h[...]).astype(BF16)
        moving = send_field(2 * t, rhb[...])
        upd[...] = sigmoid(pre[:, WIDTH:] + dot(s12[...], w12[:, WIDTH:]))
        acc[...] = dot(m[:, 0:SEG], rhb[...])
        pre[:, 0:WIDTH] = gx[t, :, 2 * WIDTH :] + dot(rhb[...], wch[0])
        if t == 0:
            x_project(1)
            x_spread(1)
        for c in moving:
            c.wait_recv()
        arrive(rhb, rh[2 * t])
        wc12 = wch[1:3].reshape(2 * WIDTH, WIDTH)
        cand = jnp.tanh(pre[:, 0:WIDTH] + dot(s12[...], wc12))
        new = cand + upd[...] * (h[...] - cand)
        h[...] = new
        hb[...] = new.astype(BF16)
        if t < LAGS - 1:
            moving = send_field(2 * t + 1, hb[...])

    out_state = pltpu.make_async_copy(hb, sf_o, out_sem.at[0])
    out_state.start()
    v = dot(hb[...], wo[...]) + bo[...]
    soft = jnp.maximum(v, 0.0) + jnp.log1p(jnp.exp(-jnp.abs(v)))
    block = 0.05 * jnp.sum(soft.reshape(NBLK, BS, WIDTH), axis=1)
    btsend[...] = block.astype(BF16)
    b_moves = []
    for k in range(1, nr):
        copy = pltpu.make_async_remote_copy(
            src_ref=btsend, dst_ref=btrecv.at[k],
            send_sem=b_send.at[k], recv_sem=b_recv.at[k],
            device_id={"region": peers[k]}, device_id_type=MESH,
        )
        copy.start()
        b_moves.append(copy)
    btrecv[0] = btsend[...]
    for c in c_moves:
        c.wait_recv()
    for plane in range(2):
        for j in range(own_hi):
            part = crecv[:, plane, j * NBLK : (j + 1) * NBLK, :].reshape(nr * NBLK, WIDTH)
            ct[plane, j * WIDTH : (j + 1) * WIDTH, :] = jnp.transpose(part)
    for c in b_moves:
        c.wait_recv()
    times = btrecv[...].reshape(nr * NBLK, WIDTH)
    ptv[...] = dot(ct[0], times) + dot(ct[1], times)
    out_path = pltpu.make_async_copy(ptv, pt_o, out_sem.at[1])
    out_path.start()
    for c in sends + c_moves + b_moves:
        c.wait_send()
    out_state.wait()
    out_path.wait()


def solution(mesh):
    nr, nd = mesh.shape["region"], mesh.shape["dom"]
    owned = PATHS // nr
    own_rows = SLOT_HI // nr * NBLK
    vmem = pltpu.VMEM
    scratch = [
        vmem((4, SEG), jnp.int32), vmem((4, SEG), F32), vmem((1, 2 * BND), jnp.int32),
        vmem((SEG, LAGS * WIDTH), BF16),
        vmem((3, WIDTH, 3 * WIDTH), BF16), vmem((3, WIDTH, 2 * WIDTH), BF16), vmem((3, WIDTH, WIDTH), BF16),
        vmem((WIDTH, WIDTH), BF16),
        vmem((1, 2 * WIDTH), F32), vmem((1, WIDTH), F32), vmem((1, WIDTH), F32),
        vmem((1, ENT), jnp.int32), vmem((1, ENT), jnp.int32), vmem((SLOT_HI, WIDTH), jnp.int32),
        vmem((SEG, WIDTH), F32), vmem((SEG, WIDTH), BF16), vmem((SEG, WIDTH), BF16),
        vmem((2 * SEG, SEG + 2 * WIDTH), BF16), vmem((SEG, WIDTH), BF16), vmem((WIDTH, SEG), BF16),
        vmem((WIDTH, SEG), BF16), vmem((SEG, SEG + 2 * WIDTH), F32), vmem((WIDTH, SEG + 2 * WIDTH), BF16),
        vmem((2 * SEG, WIDTH), F32), vmem((SEG, 2 * WIDTH), BF16), vmem((2, 2 * SEG, 2 * WIDTH), BF16),
        vmem((LAGS, SEG, 3 * WIDTH), F32), vmem((SEG, 2 * WIDTH), F32), vmem((SEG, WIDTH), F32),
        vmem((128, 256), BF16), vmem((256, 256), BF16),
        vmem((2, 128, 256), BF16), vmem((2, 256, 256), BF16),
        vmem((2 * LAGS - 1, 128, WIDTH), BF16), vmem((2 * LAGS - 1, 256, WIDTH), BF16),
        vmem((2, SLOT_HI * NBLK, WIDTH), BF16), vmem((nr, 2, own_rows, WIDTH), BF16),
        vmem((2, owned, nr * NBLK), BF16),
        vmem((NBLK, WIDTH), BF16), vmem((nr, NBLK, WIDTH), BF16), vmem((owned, WIDTH), F32),
        pltpu.SemaphoreType.DMA((16,)),
        pltpu.SemaphoreType.DMA((2 + 2 * LAGS, 4)), pltpu.SemaphoreType.DMA((2 + 2 * LAGS, 4)),
        pltpu.SemaphoreType.DMA((nr,)), pltpu.SemaphoreType.DMA((nr,)),
        pltpu.SemaphoreType.DMA((nr,)), pltpu.SemaphoreType.DMA((nr,)),
        pltpu.SemaphoreType.DMA((2,)),
    ]
    call = pl.pallas_call(
        functools.partial(kernel, nr, nd),
        out_shape=(
            jax.ShapeDtypeStruct((SEG, WIDTH), BF16),
            jax.ShapeDtypeStruct((owned, WIDTH), F32),
        ),
        in_specs=[pl.BlockSpec(memory_space=pl.ANY)] * 14,
        out_specs=(pl.BlockSpec(memory_space=pl.ANY), pl.BlockSpec(memory_space=pl.ANY)),
        scratch_shapes=scratch,
        compiler_params=pltpu.CompilerParams(
            collective_id=0, has_side_effects=True, vmem_limit_bytes=40 * 1024 * 1024
        ),
        cost_estimate=pl.CostEstimate(flops=6 * 10**9, bytes_accessed=2 * 10**6, transcendentals=10**6),
    )

    def per_device(
        inputs, state_init, neighbors, edge_weight, boundary, w_gate, b_gate, w_cand, b_cand,
        w_out, b_out, inc_block, inc_path, path_slot,
    ):
        state, paths = call(
            jnp.transpose(neighbors), jnp.transpose(edge_weight), boundary.reshape(1, -1),
            state_init, inputs, w_gate, w_cand, w_out,
            b_gate.reshape(1, -1), b_cand.reshape(1, -1), b_out.reshape(1, -1),
            inc_block.reshape(1, -1), inc_path.reshape(1, -1), path_slot.reshape(SLOT_HI, WIDTH),
        )
        return state, paths[None]

    both = ("region", "dom")
    placed = (
        P(both, None), P(both, None), P(both, None), P(both, None), P(both),
        P(), P(), P(), P(), P(), P(), P(both), P(both), P("dom", None),
    )
    return jax.shard_map(
        per_device,
        mesh=mesh,
        in_specs=placed,
        out_specs=(P(both, None), P("dom", "region", None)),
        check_vma=False,
    )
```

time: 259 us -> 78.2 us (0.30)
  the two profiles are of different devices: /device:TPU:25 before, /device:TPU:1 now
where the time goes in v1:
time: 78.2 us; the launch traced here: 77.8 us
  Pallas kernels  66.4 us (85%)
  local copies, waits for them, and re-layouts  10.7 us (14%)
    pallas_call x1, Pallas kernels, per_device(): call(jnp.transpose(neighbors), jnp.transpose(edge_weight), boundary.resha...  66.4 us
    unnamed x30, local copies, waits for them, and re-layouts  10.7 us

profile of v1, /device:TPU:1, one launch (start us, length us, event | category | flops | bytes accessed | tf_op | source)
XLA Modules:
  0.0 77.8 jit_solution(12307226765641792832)
XLA Ops:
  0.6 0.0 copy-start.6
  0.6 0.0 copy-start.5
  0.7 0.0 copy-start.10
  0.7 0.7 copy-done.6
  1.3 0.0 copy-done.5
  1.4 0.0 copy-done.10
  1.4 0.0 copy-start
  1.4 1.0 %copy-done = bf16[512,512]{1,0:T(8,128)(2,1)S(1)} copy-done((bf16[512,512]{1,0:T(8,128)(2,1)S(1)}, bf16[512,512]{1,0:T(8,128)(2,1)}, u32[]{:S(2)}) %copy-start) | copy-done | bytes 524312
  2.4 0.0 copy-start.1
  2.4 1.0 %copy-done.1 = bf16[3,256,256]{2,1,0:T(8,128)(2,1)S(1)} copy-done((bf16[3,256,256]{2,1,0:T(8,128)(2,1)S(1)}, bf16[3,256,256]{2,1,0:T(8,128)(2,1)}, u32[]{:S(2)}) %copy-start.1) | copy-done | bytes 393240
  3.4 0.0 copy-start.2
  3.4 0.9 %copy-done.2 = bf16[3,256,128]{2,1,0:T(8,128)(2,1)S(1)} copy-done((bf16[3,256,128]{2,1,0:T(8,128)(2,1)S(1)}, bf16[3,256,128]{2,1,0:T(8,128)(2,1)}, u32[]{:S(2)}) %copy-start.2) | copy-done | bytes 196632
  4.3 0.0 copy-start.3
  4.3 0.9 %copy-done.3 = bf16[512,128]{1,0:T(8,128)(2,1)S(1)} copy-done((bf16[512,128]{1,0:T(8,128)(2,1)S(1)}, bf16[512,128]{1,0:T(8,128)(2,1)}, u32[]{:S(2)}) %copy-start.3) | copy-done | bytes 131096
  5.2 0.0 copy-start.4
  5.2 0.8 copy-done.4
  6.0 0.0 copy-start.7
  6.0 0.7 copy-done.7
  6.7 0.0 copy-start.8
  6.7 0.7 copy-done.8
  7.4 0.0 copy-start.9
  7.4 0.7 copy-done.9
  8.1 0.0 copy-start.11
  8.1 0.7 copy-done.11
  8.7 0.0 copy-start.12
  8.7 0.7 copy-done.12
  9.4 0.0 copy-start.13
  9.4 0.7 copy-done.13
  10.0 66.4 %shard_map.149 = (bf16[512,128]{1,0:T(8,128)(2,1)S(1)}, f32[256,128]{1,0:T(8,128)S(1)}) custom-call(s32[4,512]{1,0:T(4,128)S(1)} %bitcast.11, f32[4,512]{1,0:T(4,128)S(1)} %bitcast.12, s32[1,64]{1,0:T(1,128)S(1)} %bitcast.17, bf16[512,128]{1,0:T(8,128)(2,1)S(1)} %copy-done.3, bf16[512,512]{1,0:T(8,128)(2,1)S(1)} %copy-done, ...), custom_call_target="tpu_custom_call" | custom-call | flops 6000000000 | bytes 2000000 | tf_op jit(solution)/shard_map/pallas_call | solution.py:349
  76.4 0.7 copy.18
  77.1 0.7 copy.19
Async XLA Ops:
  0.6 0.7 copy-start.6
  0.6 0.7 copy-start.5
  0.7 0.7 copy-start.10
  1.4 1.0 %copy-start = (bf16[512,512]{1,0:T(8,128)(2,1)S(1)}, bf16[512,512]{1,0:T(8,128)(2,1)}, u32[]{:S(2)}) copy-start(bf16[512,512]{1,0:T(8,128)(2,1)} %x_h.1) | copy-start | bytes 1572868
  2.4 1.0 %copy-start.1 = (bf16[3,256,256]{2,1,0:T(8,128)(2,1)S(1)}, bf16[3,256,256]{2,1,0:T(8,128)(2,1)}, u32[]{:S(2)}) copy-start(bf16[3,256,256]{2,1,0:T(8,128)(2,1)} %wg_h.1) | copy-start | bytes 1179652
  3.4 0.9 %copy-start.2 = (bf16[3,256,128]{2,1,0:T(8,128)(2,1)S(1)}, bf16[3,256,128]{2,1,0:T(8,128)(2,1)}, u32[]{:S(2)}) copy-start(bf16[3,256,128]{2,1,0:T(8,128)(2,1)} %wc_h.1) | copy-start | bytes 589828
  4.3 0.9 %copy-start.3 = (bf16[512,128]{1,0:T(8,128)(2,1)S(1)}, bf16[512,128]{1,0:T(8,128)(2,1)}, u32[]{:S(2)}) copy-start(bf16[512,128]{1,0:T(8,128)(2,1)} %h0_h.1) | copy-start | bytes 393220
  5.2 0.8 copy-start.4
  6.0 0.7 copy-start.7
  6.7 0.7 copy-start.8
  7.4 0.7 copy-start.9
  8.1 0.7 copy-start.11
  8.7 0.7 copy-start.12
  9.4 0.7 copy-start.13

commit v2 on v1

--- a/solution.py
+++ b/solution.py
@@ -33,12 +33,19 @@
     nbr, ew, bnd, x, wx, wgh, wch, wo, bg, bc, bo, ib, ip, ps,
     h, hb, rhb, m, ar, pk, s, aa, g, acc, s12, sx, gx, pre, upd,
     e0, r0, ex, rx, eh, rh,
-    cnt, crecv, ct, btsend, btrecv, ptv,
-    load_sem, send_sem, recv_sem, c_send, c_recv, b_send, b_recv, out_sem,
+    cnt, crecv, ct, btsend, btrecv,
+    load_sem, send_sem, recv_sem, c_send, c_recv, b_send, b_recv,
 ):
     region, dom = lax.axis_index("region"), lax.axis_index("dom")
-    up1, dn1 = lax.rem(dom + 1, nd), lax.rem(dom + nd - 1, nd)
-    up2, dn2 = lax.rem(dom + 2, nd), lax.rem(dom + nd - 2, nd)
+    hops = (1, -1, 2, -2)
+    valid = [dom + hop < nd if hop > 0 else dom + hop >= 0 for hop in hops]
+    source = [valid[1], valid[0], valid[3], valid[2]]
+    guests = sum(v.astype(jnp.int32) for v in valid)
+
+    def to_each(act):
+        for j in (2, 3, 0, 1):
+            pl.when(valid[j])(functools.partial(act, j, {"dom": dom + hops[j]}))
+
     peers = [None] + [lax.rem(region + k, nr) for k in range(1, nr)]
     own_hi = SLOT_HI // nr
     own_rows = own_hi * NBLK
@@ -51,7 +58,7 @@
         loads.append(copy)
         return copy
 
-    l_graph = [load(nbr_h, nbr), load(ew_h, ew), load(bnd_h, bnd)]
+    l_graph = [load(nbr_h, nbr.at[0:4]), load(ew_h, ew.at[0:4]), load(bnd_h, bnd)]
     l_h0 = load(h0_h, hb)
     l_x = load(x_h, x)
     l_path = [load(ib_h, ib), load(ip_h, ip), load(ps_h, ps)]
@@ -66,9 +73,18 @@
         load(bo_h, bo),
     ]
 
+    r0[192:256, :] = jnp.zeros((64, 256), BF16)
+    rx[:, 192:256, :] = jnp.zeros((2, 64, 256), BF16)
+    rh[:, 192:256, :] = jnp.zeros((2 * LAGS - 1, 64, WIDTH), BF16)
+
+    @pl.when((dom < 2) | (dom >= nd - 2))
+    def _():
+        r0[0:192, :] = jnp.zeros((192, 256), BF16)
+        rx[:, 0:192, :] = jnp.zeros((2, 192, 256), BF16)
+        rh[:, 0:192, :] = jnp.zeros((2 * LAGS - 1, 192, WIDTH), BF16)
+
     barrier = pltpu.get_barrier_semaphore()
-    for there in (up1, dn1, up2, dn2):
-        pl.semaphore_signal(barrier, inc=1, device_id={"dom": there}, device_id_type=MESH)
+    to_each(lambda j, there: pl.semaphore_signal(barrier, inc=1, device_id=there, device_id_type=MESH))
     for k in range(1, nr):
         pl.semaphore_signal(barrier, inc=1, device_id={"region": peers[k]}, device_id_type=MESH)
 
@@ -79,15 +95,14 @@
         (dom == nd - 1) & (near >= SEG + BND)
     )
     near = jnp.where(outside, -1, near).astype(F32)
-    raw = ew[...]
-    wts = raw / jnp.sum(raw, axis=0, keepdims=True)
-    tall = jnp.transpose(jnp.concatenate([near, wts], axis=0))
+    wts = ew[...] / (ew[0:1, :] + ew[1:2, :] + ew[2:3, :] + ew[3:4, :])
+    rows, tall = jnp.transpose(near), jnp.transpose(wts)
     step = 32
     lanes = iota((step, SEG + WIDTH), 1).astype(F32)
     for i in range(0, SEG, step):
         a = jnp.zeros((step, SEG + WIDTH), F32)
         for k in range(4):
-            a = a + jnp.where(lanes == tall[i : i + step, k : k + 1], tall[i : i + step, 4 + k : 5 + k], 0.0)
+            a = a + jnp.where(lanes == rows[i : i + step, k : k + 1], tall[i : i + step, k : k + 1], 0.0)
         a = a.astype(BF16)
         m[i : i + step, 0:SEG] = a[:, 0:SEG]
         ar[i : i + step, :] = a[:, SEG:]
@@ -105,40 +120,38 @@
 
     sends = []
 
-    def exchange(n, src, dst, far):
-        lo, hi = far
-        plan = (
-            (src.at[0:64], dst.at[0:64], up1),
-            (src.at[64:128], dst.at[64:128], dn1),
-            (src.at[0:32, lo:hi], dst.at[128:160, lo:hi], up2),
-            (src.at[64:96, lo:hi], dst.at[160:192, lo:hi], dn2),
-        )
-        copies = []
-        for j, (a, b, there) in enumerate(plan):
-            copy = pltpu.make_async_remote_copy(
-                src_ref=a, dst_ref=b, send_sem=send_sem.at[n, j], recv_sem=recv_sem.at[n, j],
-                device_id={"dom": there}, device_id_type=MESH,
+    def exchange(n, src, dst, width, far_width):
+        def move(j, there):
+            first, size = (0, 64)[j % 2], (64, 32)[j // 2]
+            base = (0, 64, 128, 160)[j]
+            cols = slice(0, far_width if j >= 2 else width)
+            return pltpu.make_async_remote_copy(
+                src_ref=src.at[first : first + size, cols], dst_ref=dst.at[base : base + size, cols],
+                send_sem=send_sem.at[n, j], recv_sem=recv_sem.at[n, j],
+                device_id=there, device_id_type=MESH,
             )
-            copy.start()
-            copies.append(copy)
-        sends.extend(copies)
-        return copies
+
+        to_each(lambda j, there: move(j, there).start())
+        moves = [move(j, {"dom": lax.rem(dom + 1, nd)}) for j in range(4)]
+        sends.extend(enumerate(moves))
+        return moves
+
+    def received(moves, which):
+        for j in which:
+            pl.when(source[j])(moves[j].wait_recv)
 
     l_h0.wait()
     e0[:, 0:WIDTH] = dot(s[...], hb[...]).astype(BF16)
     e0[:, WIDTH:] = dot(s[...], ar[...]).astype(BF16)
-    pl.semaphore_wait(barrier, 4 + nr - 1)
-    first = exchange(0, e0, r0, (0, WIDTH))
+    pl.semaphore_wait(barrier, guests + nr - 1)
+    first = exchange(0, e0, r0, 256, WIDTH)
     l_x.wait()
     x_moves = []
     for pair in range(2):
         cols = slice(pair * 256, pair * 256 + 256)
         ex[pair] = dot(s[...], x[:, cols]).astype(BF16)
-        x_moves.append(exchange(1 + pair, ex.at[pair], rx.at[pair], (0, 256)))
-
-    r0[192:256, :] = jnp.zeros((64, 256), BF16)
-    rx[:, 192:256, :] = jnp.zeros((2, 64, 256), BF16)
-    rh[:, 192:256, :] = jnp.zeros((2 * LAGS - 1, 64, WIDTH), BF16)
+        x_moves.append(exchange(1 + pair, ex.at[pair], rx.at[pair], 256, 256))
+
     row, col = iota((WIDTH, 2 * WIDTH), 0), iota((WIDTH, 2 * WIDTH), 1)
     place = ((row < 32) & (col == row)) | ((row >= 32) & (row < 64) & (col == row + 32))
     m[0:SEG, SEG:] = dot(ar[...], place.astype(F32).astype(BF16)).astype(BF16)
@@ -182,8 +195,7 @@
         c_moves.append(copy)
     crecv[0] = cnt[:, pl.ds(pl.multiple_of(region * own_rows, own_rows), own_rows), :]
 
-    for c in first:
-        c.wait_recv()
+    received(first, range(4))
     lane = iota((32, WIDTH), 1)
     b_low, b_up = r0[0:32, WIDTH:].astype(F32), r0[64:96, WIDTH:].astype(F32)
     g_row, g_col = iota((32, WIDTH), 0), iota((32, WIDTH), 1)
@@ -203,8 +215,7 @@
 
     def x_spread(pair):
         cols = slice(pair * 256, pair * 256 + 256)
-        for c in x_moves[pair]:
-            c.wait_recv()
+        received(x_moves[pair], range(4))
         sx[pair] = (dot(m[:, 0:SEG], x[:, cols]) + dot(m[:, SEG:], rx[pair])).astype(BF16)
 
     def x_project(t):
@@ -217,14 +228,19 @@
             + bias
         )
 
-    def arrive(field, recv):
-        both = acc[...] + dot(m[:, SEG:], recv)
-        s12[:, 0:WIDTH] = both[0:SEG].astype(BF16)
-        s12[:, WIDTH:] = both[SEG:].astype(BF16)
+    def arrive(moves, recv):
+        if moves is not None:
+            received(moves, (0, 1))
+        near = acc[...] + dot(m[:, SEG : SEG + WIDTH], recv[0:128])
+        s12[:, 0:WIDTH] = near[0:SEG].astype(BF16)
+        if moves is not None:
+            received(moves, (2, 3))
+        far = near[SEG:] + dot(m[SEG:, SEG + WIDTH :], recv[128:256])
+        s12[:, WIDTH:] = far.astype(BF16)
 
     def send_field(n, field):
         eh[n] = dot(s[...], field).astype(BF16)
-        return exchange(3 + n, eh.at[n], rh.at[n], (0, WIDTH))
+        return exchange(3 + n, eh.at[n], rh.at[n], WIDTH, WIDTH)
 
     h[...] = hb[...].astype(F32)
     x_spread(0)
@@ -238,11 +254,9 @@
         if t == 2:
             x_project(3)
         if t == 0:
-            arrive(hb, r0[:, 0:WIDTH])
+            arrive(None, r0.at[:, 0:WIDTH])
         else:
-            for c in moving:
-                c.wait_recv()
-            arrive(hb, rh[2 * t - 1])
+            arrive(moving, rh.at[2 * t - 1])
         w12 = wgh[1:3].reshape(2 * WIDTH, 2 * WIDTH)
         reset = sigmoid(pre[:, 0:WIDTH] + dot(s12[...], w12[:, 0:WIDTH]))
         rhb[...] = (reset * h[...]).astype(BF16)
@@ -253,20 +267,16 @@
         if t == 0:
             x_project(1)
             x_spread(1)
-        for c in moving:
-            c.wait_recv()
-        arrive(rhb, rh[2 * t])
+        arrive(moving, rh.at[2 * t])
         wc12 = wch[1:3].reshape(2 * WIDTH, WIDTH)
         cand = jnp.tanh(pre[:, 0:WIDTH] + dot(s12[...], wc12))
         new = cand + upd[...] * (h[...] - cand)
         h[...] = new
-        hb[...] = new.astype(BF16)
+        (hb if t < LAGS - 1 else sf_o)[...] = new.astype(BF16)
         if t < LAGS - 1:
             moving = send_field(2 * t + 1, hb[...])
 
-    out_state = pltpu.make_async_copy(hb, sf_o, out_sem.at[0])
-    out_state.start()
-    v = dot(hb[...], wo[...]) + bo[...]
+    v = dot(sf_o[...], wo[...]) + bo[...]
     soft = jnp.maximum(v, 0.0) + jnp.log1p(jnp.exp(-jnp.abs(v)))
     block = 0.05 * jnp.sum(soft.reshape(NBLK, BS, WIDTH), axis=1)
     btsend[...] = block.astype(BF16)
@@ -289,13 +299,11 @@
     for c in b_moves:
         c.wait_recv()
     times = btrecv[...].reshape(nr * NBLK, WIDTH)
-    ptv[...] = dot(ct[0], times) + dot(ct[1], times)
-    out_path = pltpu.make_async_copy(ptv, pt_o, out_sem.at[1])
-    out_path.start()
-    for c in sends + c_moves + b_moves:
+    pt_o[...] = dot(ct[0], times) + dot(ct[1], times)
+    for j, c in sends:
+        pl.when(valid[j])(c.wait_send)
+    for c in c_moves + b_moves:
         c.wait_send()
-    out_state.wait()
-    out_path.wait()
 
 
 def solution(mesh):
@@ -304,7 +312,7 @@
     own_rows = SLOT_HI // nr * NBLK
     vmem = pltpu.VMEM
     scratch = [
-        vmem((4, SEG), jnp.int32), vmem((4, SEG), F32), vmem((1, 2 * BND), jnp.int32),
+        vmem((8, SEG), jnp.int32), vmem((8, SEG), F32), vmem((1, 2 * BND), jnp.int32),
         vmem((SEG, LAGS * WIDTH), BF16),
         vmem((3, WIDTH, 3 * WIDTH), BF16), vmem((3, WIDTH, 2 * WIDTH), BF16), vmem((3, WIDTH, WIDTH), BF16),
         vmem((WIDTH, WIDTH), BF16),
@@ -320,24 +328,23 @@
         vmem((2 * LAGS - 1, 128, WIDTH), BF16), vmem((2 * LAGS - 1, 256, WIDTH), BF16),
         vmem((2, SLOT_HI * NBLK, WIDTH), BF16), vmem((nr, 2, own_rows, WIDTH), BF16),
         vmem((2, owned, nr * NBLK), BF16),
-        vmem((NBLK, WIDTH), BF16), vmem((nr, NBLK, WIDTH), BF16), vmem((owned, WIDTH), F32),
+        vmem((NBLK, WIDTH), BF16), vmem((nr, NBLK, WIDTH), BF16),
         pltpu.SemaphoreType.DMA((16,)),
         pltpu.SemaphoreType.DMA((2 + 2 * LAGS, 4)), pltpu.SemaphoreType.DMA((2 + 2 * LAGS, 4)),
         pltpu.SemaphoreType.DMA((nr,)), pltpu.SemaphoreType.DMA((nr,)),
         pltpu.SemaphoreType.DMA((nr,)), pltpu.SemaphoreType.DMA((nr,)),
-        pltpu.SemaphoreType.DMA((2,)),
     ]
     call = pl.pallas_call(
         functools.partial(kernel, nr, nd),
         out_shape=(
-            jax.ShapeDtypeStruct((SEG, WIDTH), BF16),
-            jax.ShapeDtypeStruct((owned, WIDTH), F32),
+            vmem((SEG, WIDTH), BF16),
+            vmem((owned, WIDTH), F32),
         ),
         in_specs=[pl.BlockSpec(memory_space=pl.ANY)] * 14,
-        out_specs=(pl.BlockSpec(memory_space=pl.ANY), pl.BlockSpec(memory_space=pl.ANY)),
+        out_specs=(pl.BlockSpec(memory_space=pltpu.VMEM), pl.BlockSpec(memory_space=pltpu.VMEM)),
         scratch_shapes=scratch,
         compiler_params=pltpu.CompilerParams(
-            collective_id=0, has_side_effects=True, vmem_limit_bytes=40 * 1024 * 1024
+            collective_id=0, has_side_effects=True, vmem_limit_bytes=56 * 1024 * 1024
         ),
         cost_estimate=pl.CostEstimate(flops=6 * 10**9, bytes_accessed=2 * 10**6, transcendentals=10**6),
     )

time: 78.2 us -> 56.7 us (0.73)
  the two profiles are of different devices: /device:TPU:1 before, /device:TPU:25 now
where the time goes in v2:
time: 56.7 us; the launch traced here: 56.6 us
  Pallas kernels  54.6 us (96%)
  local copies, waits for them, and re-layouts  1.31 us (2%)
  between operations  0.64 us (1%)
    pallas_call x1, Pallas kernels, per_device(): call(jnp.transpose(neighbors), jnp.transpose(edge_weight), boundary.resha...  54.6 us
    unnamed x2, local copies, waits for them, and re-layouts  1.31 us

profile of v2, /device:TPU:25, one launch (start us, length us, event | category | flops | bytes accessed | tf_op | source)
XLA Modules:
  0.0 56.6 jit_solution(4091154917870984534)
XLA Ops:
  0.6 54.6 %shard_map.149 = (bf16[512,128]{1,0:T(8,128)(2,1)S(1)}, f32[256,128]{1,0:T(8,128)S(1)}) custom-call(s32[4,512]{1,0:T(4,128)} %bitcast.11, f32[4,512]{1,0:T(4,128)} %bitcast.12, s32[1,64]{1,0:T(1,128)} %bitcast.17, bf16[512,128]{1,0:T(8,128)(2,1)} %h0_h.1, bf16[512,512]{1,0:T(8,128)(2,1)} %x_h.1, bf16[3,256,256]{2,1,0:T(8,128)(2,1)} %wg_h.1, ...), custom_call_target="tpu_custom_call" | custom-call | flops 6000000000 | bytes 2000000 | tf_op jit(solution)/shard_map/pallas_call | solution.py:356
  55.3 0.7 %copy.18 = bf16[512,128]{1,0:T(8,128)(2,1)} copy(bf16[512,128]{1,0:T(8,128)(2,1)S(1)} %get-tuple-element.6) | data formatting | bytes 262144
  55.9 0.7 %copy.19 = f32[1,256,128]{2,1,0:T(8,128)} copy(f32[1,256,128]{2,1,0:T(8,128)S(1)} %bitcast.10) | data formatting | bytes 262144

commit v3 on v2

--- a/solution.py
+++ b/solution.py
@@ -31,7 +31,7 @@
     nbr_h, ew_h, bnd_h, h0_h, x_h, wg_h, wc_h, wo_h, bg_h, bc_h, bo_h, ib_h, ip_h, ps_h,
     sf_o, pt_o,
     nbr, ew, bnd, x, wx, wgh, wch, wo, bg, bc, bo, ib, ip, ps,
-    h, hb, rhb, m, ar, pk, s, aa, g, acc, s12, sx, gx, pre, upd,
+    h, hb, rhb, m, ar, pk, s, aa, g, s12, sx, gx, pre, upd,
     e0, r0, ex, rx, eh, rh,
     cnt, crecv, ct, btsend, btrecv,
     load_sem, send_sem, recv_sem, c_send, c_recv, b_send, b_recv,
@@ -73,15 +73,14 @@
         load(bo_h, bo),
     ]
 
-    r0[192:256, :] = jnp.zeros((64, 256), BF16)
+    r0[192:256, :] = jnp.zeros((64, 3 * WIDTH), BF16)
     rx[:, 192:256, :] = jnp.zeros((2, 64, 256), BF16)
-    rh[:, 192:256, :] = jnp.zeros((2 * LAGS - 1, 64, WIDTH), BF16)
 
     @pl.when((dom < 2) | (dom >= nd - 2))
     def _():
-        r0[0:192, :] = jnp.zeros((192, 256), BF16)
+        r0[0:192, :] = jnp.zeros((192, 3 * WIDTH), BF16)
         rx[:, 0:192, :] = jnp.zeros((2, 192, 256), BF16)
-        rh[:, 0:192, :] = jnp.zeros((2 * LAGS - 1, 192, WIDTH), BF16)
+        rh[...] = jnp.zeros((2 * LAGS - 1, 192, WIDTH), BF16)
 
     barrier = pltpu.get_barrier_semaphore()
     to_each(lambda j, there: pl.semaphore_signal(barrier, inc=1, device_id=there, device_id_type=MESH))
@@ -94,29 +93,28 @@
     outside = ((dom == 0) & (near >= SEG) & (near < SEG + BND)) | (
         (dom == nd - 1) & (near >= SEG + BND)
     )
-    near = jnp.where(outside, -1, near).astype(F32)
+    near = jnp.where(outside, -1, near)
     wts = ew[...] / (ew[0:1, :] + ew[1:2, :] + ew[2:3, :] + ew[3:4, :])
-    rows, tall = jnp.transpose(near), jnp.transpose(wts)
-    step = 32
-    lanes = iota((step, SEG + WIDTH), 1).astype(F32)
-    for i in range(0, SEG, step):
-        a = jnp.zeros((step, SEG + WIDTH), F32)
-        for k in range(4):
-            a = a + jnp.where(lanes == rows[i : i + step, k : k + 1], tall[i : i + step, k : k + 1], 0.0)
-        a = a.astype(BF16)
-        m[i : i + step, 0:SEG] = a[:, 0:SEG]
-        ar[i : i + step, :] = a[:, SEG:]
-
     turn = lax.rem(iota((2 * BND, 2 * BND), 0) + BND, 2 * BND) == iota((2 * BND, 2 * BND), 1)
     picked = jnp.sum(jnp.where(turn, bnd[...].astype(F32), 0.0), axis=1, keepdims=True)
     picker = (iota((2 * BND, SEG), 1).astype(F32) == picked).astype(F32).astype(BF16)
     pk[0 : 2 * BND, :] = picker
     pk[2 * BND :, :] = jnp.zeros((2 * BND, SEG), BF16)
-    a_bnd = dot(picker, m[0:SEG, 0:SEG]).astype(BF16)
+    w_top = wts.astype(BF16).astype(F32)
+    edges = jnp.concatenate(
+        [lax.shift_right_arithmetic(near, 3).astype(F32), (near & 7).astype(F32), w_top, wts - w_top], axis=0
+    ).astype(BF16)
+    chosen = lax.dot_general(picker, edges, (((1,), (1,)), ((), ())), preferred_element_type=F32)
+    at = iota((2 * BND, SEG + WIDTH), 1).astype(F32)
+    a_bnd = jnp.zeros((2 * BND, SEG + WIDTH), F32)
+    for k in range(4):
+        row_at = 8.0 * chosen[:, k : k + 1] + chosen[:, 8 + k : 9 + k]
+        a_bnd = a_bnd + jnp.where(at == row_at, chosen[:, 16 + k : 17 + k] + chosen[:, 24 + k : 25 + k], 0.0)
+    a_bnd = a_bnd.astype(BF16)
     s[0:32, :] = picker[0:32]
-    s[32:64, :] = a_bnd[0:32]
+    s[32:64, :] = a_bnd[0:32, 0:SEG]
     s[64:96, :] = picker[32:64]
-    s[96:128, :] = a_bnd[32:64]
+    s[96:128, :] = a_bnd[32:64, 0:SEG]
 
     sends = []
 
@@ -142,15 +140,29 @@
 
     l_h0.wait()
     e0[:, 0:WIDTH] = dot(s[...], hb[...]).astype(BF16)
-    e0[:, WIDTH:] = dot(s[...], ar[...]).astype(BF16)
+    e0[0:32, 2 * WIDTH :] = a_bnd[0:32, SEG:]
+    e0[32:64, 2 * WIDTH :] = jnp.zeros((32, WIDTH), BF16)
+    e0[64:96, 2 * WIDTH :] = a_bnd[32:64, SEG:]
+    e0[96:128, 2 * WIDTH :] = jnp.zeros((32, WIDTH), BF16)
+    l_x.wait()
+    e0[:, WIDTH : 2 * WIDTH] = dot(s[...], x[:, 0:WIDTH]).astype(BF16)
     pl.semaphore_wait(barrier, guests + nr - 1)
-    first = exchange(0, e0, r0, 256, WIDTH)
-    l_x.wait()
+    first = exchange(0, e0, r0, 3 * WIDTH, 2 * WIDTH)
     x_moves = []
-    for pair in range(2):
-        cols = slice(pair * 256, pair * 256 + 256)
-        ex[pair] = dot(s[...], x[:, cols]).astype(BF16)
-        x_moves.append(exchange(1 + pair, ex.at[pair], rx.at[pair], 256, 256))
+    for part, (low, wide) in enumerate(((WIDTH, 2 * WIDTH), (3 * WIDTH, WIDTH))):
+        ex[part, :, 0:wide] = dot(s[...], x[:, low : low + wide]).astype(BF16)
+        x_moves.append(exchange(1 + part, ex.at[part], rx.at[part], wide, wide))
+
+    rows, tall = jnp.transpose(near.astype(F32)), jnp.transpose(wts)
+    step = 32
+    lanes = iota((step, SEG + WIDTH), 1).astype(F32)
+    for i in range(0, SEG, step):
+        a = jnp.zeros((step, SEG + WIDTH), F32)
+        for k in range(4):
+            a = a + jnp.where(lanes == rows[i : i + step, k : k + 1], tall[i : i + step, k : k + 1], 0.0)
+        a = a.astype(BF16)
+        m[i : i + step, 0:SEG] = a[:, 0:SEG]
+        ar[i : i + step, :] = a[:, SEG:]
 
     row, col = iota((WIDTH, 2 * WIDTH), 0), iota((WIDTH, 2 * WIDTH), 1)
     place = ((row < 32) & (col == row)) | ((row >= 32) & (row < 64) & (col == row + 32))
@@ -195,14 +207,20 @@
         c_moves.append(copy)
     crecv[0] = cnt[:, pl.ds(pl.multiple_of(region * own_rows, own_rows), own_rows), :]
 
+    for c in l_w:
+        c.wait()
+    bias = jnp.concatenate([bg[...], bc[...]], axis=1)
+    gx[0] = dot(x[:, 0:WIDTH], wx[0]) + bias
+
     received(first, range(4))
     lane = iota((32, WIDTH), 1)
-    b_low, b_up = r0[0:32, WIDTH:].astype(F32), r0[64:96, WIDTH:].astype(F32)
+    b_low, b_up = r0[0:32, 2 * WIDTH :].astype(F32), r0[64:96, 2 * WIDTH :].astype(F32)
     g_row, g_col = iota((32, WIDTH), 0), iota((32, WIDTH), 1)
     g[0:32, SEG : SEG + WIDTH] = (g_col == g_row + 32).astype(F32).astype(BF16)
     g[32:64, SEG : SEG + WIDTH] = (g_col == g_row + 96).astype(F32).astype(BF16)
-    g[0:32, SEG + WIDTH :] = jnp.where(lane < 32, b_low, 0.0).astype(BF16)
-    g[32:64, SEG + WIDTH :] = jnp.where((lane >= 32) & (lane < 64), b_up, 0.0).astype(BF16)
+    one_low, one_up = (lane == g_row + 64).astype(F32), (lane == g_row + 96).astype(F32)
+    g[0:32, SEG + WIDTH :] = jnp.where(lane < 32, b_low, one_low).astype(BF16)
+    g[32:64, SEG + WIDTH :] = jnp.where((lane >= 32) & (lane < 64), b_up, one_up).astype(BF16)
     back = jnp.concatenate(
         [jnp.where((lane >= 32) & (lane < 64), b_low, 0.0), jnp.where(lane < 32, b_up, 0.0)], axis=0
     ).astype(BF16)
@@ -210,66 +228,63 @@
     g[64:128, :] = jnp.zeros((64, SEG + 2 * WIDTH), BF16)
     m[SEG:, :] = (aa[...] + dot(ar[...], g[...])).astype(BF16)
 
-    for c in l_w:
-        c.wait()
-
-    def x_spread(pair):
-        cols = slice(pair * 256, pair * 256 + 256)
-        received(x_moves[pair], range(4))
-        sx[pair] = (dot(m[:, 0:SEG], x[:, cols]) + dot(m[:, SEG:], rx[pair])).astype(BF16)
+    def x_spread(part):
+        low, wide = (0, WIDTH, 3 * WIDTH)[part], (WIDTH, 2 * WIDTH, WIDTH)[part]
+        if part:
+            received(x_moves[part - 1], range(4))
+        rows = rx[part - 1, :, 0:wide] if part else r0[:, WIDTH : 2 * WIDTH]
+        both = (dot(m[:, 0:SEG], x[:, low : low + wide]) + dot(m[:, SEG:], rows)).astype(BF16)
+        for i in range(wide // WIDTH):
+            sx[low // WIDTH + i] = both[:, i * WIDTH : (i + 1) * WIDTH]
+
+    def x_direct(t):
+        gx[t] = dot(x[:, t * WIDTH : (t + 1) * WIDTH], wx[0]) + bias
 
     def x_project(t):
-        pair, cols = t // 2, slice((t % 2) * WIDTH, (t % 2 + 1) * WIDTH)
-        bias = jnp.concatenate([bg[...], bc[...]], axis=1)
-        gx[t] = (
-            dot(x[:, t * WIDTH : (t + 1) * WIDTH], wx[0])
-            + dot(sx[pair, 0:SEG, cols], wx[1])
-            + dot(sx[pair, SEG:, cols], wx[2])
-            + bias
-        )
-
-    def arrive(moves, recv):
-        if moves is not None:
-            received(moves, (0, 1))
-        near = acc[...] + dot(m[:, SEG : SEG + WIDTH], recv[0:128])
-        s12[:, 0:WIDTH] = near[0:SEG].astype(BF16)
-        if moves is not None:
-            received(moves, (2, 3))
-        far = near[SEG:] + dot(m[SEG:, SEG + WIDTH :], recv[128:256])
-        s12[:, WIDTH:] = far.astype(BF16)
+        gx[t] += dot(sx[t, 0:SEG], wx[1]) + dot(sx[t, SEG:], wx[2])
+
+    def local(field, w):
+        s12[:, 0:WIDTH] = dot(m[0:SEG, 0:SEG], field).astype(BF16)
+        s12[:, WIDTH:] = dot(m[SEG:, 0:SEG], field).astype(BF16)
+        return dot(field, w[0]) + dot(s12[...], w[1:3].reshape(2 * WIDTH, w.shape[2]))
+
+    def remote(recv, w1, w2):
+        bounds = jnp.concatenate([recv[0:32], recv[64:96]], axis=0)
+        q = jnp.concatenate([dot(recv[0:192], w2), dot(bounds, w1)], axis=0).astype(BF16)
+        return dot(m[SEG:, SEG:], q)
 
     def send_field(n, field):
         eh[n] = dot(s[...], field).astype(BF16)
         return exchange(3 + n, eh.at[n], rh.at[n], WIDTH, WIDTH)
 
-    h[...] = hb[...].astype(F32)
     x_spread(0)
     x_project(0)
-    moving = None
+    h[...] = hb[...].astype(F32)
+    moving, recv = None, r0.at[:, 0:WIDTH]
     for t in range(LAGS):
-        acc[...] = dot(m[:, 0:SEG], hb[...])
-        pre[...] = gx[t, :, 0 : 2 * WIDTH] + dot(hb[...], wgh[0])
+        pre[...] = gx[t, :, 0 : 2 * WIDTH] + local(hb[...], wgh)
+        if t == 1:
+            x_spread(2)
+            x_direct(2)
+        if t == 2:
+            x_project(3)
+        if t > 0:
+            received(moving, range(4))
+            recv = rh.at[2 * t - 1]
+        reset = sigmoid(pre[:, 0:WIDTH] + remote(recv, wgh[1, :, 0:WIDTH], wgh[2, :, 0:WIDTH]))
+        rhb[...] = (reset * h[...]).astype(BF16)
+        moving = send_field(2 * t, rhb[...])
+        upd[...] = sigmoid(pre[:, WIDTH:] + remote(recv, wgh[1, :, WIDTH:], wgh[2, :, WIDTH:]))
+        pre[:, 0:WIDTH] = gx[t, :, 2 * WIDTH :] + local(rhb[...], wch)
+        if t == 0:
+            x_spread(1)
+            x_direct(1)
+            x_project(1)
         if t == 1:
             x_project(2)
-        if t == 2:
-            x_project(3)
-        if t == 0:
-            arrive(None, r0.at[:, 0:WIDTH])
-        else:
-            arrive(moving, rh.at[2 * t - 1])
-        w12 = wgh[1:3].reshape(2 * WIDTH, 2 * WIDTH)
-        reset = sigmoid(pre[:, 0:WIDTH] + dot(s12[...], w12[:, 0:WIDTH]))
-        rhb[...] = (reset * h[...]).astype(BF16)
-        moving = send_field(2 * t, rhb[...])
-        upd[...] = sigmoid(pre[:, WIDTH:] + dot(s12[...], w12[:, WIDTH:]))
-        acc[...] = dot(m[:, 0:SEG], rhb[...])
-        pre[:, 0:WIDTH] = gx[t, :, 2 * WIDTH :] + dot(rhb[...], wch[0])
-        if t == 0:
-            x_project(1)
-            x_spread(1)
-        arrive(moving, rh.at[2 * t])
-        wc12 = wch[1:3].reshape(2 * WIDTH, WIDTH)
-        cand = jnp.tanh(pre[:, 0:WIDTH] + dot(s12[...], wc12))
+            x_direct(3)
+        received(moving, range(4))
+        cand = jnp.tanh(pre[:, 0:WIDTH] + remote(rh.at[2 * t], wch[1], wch[2]))
         new = cand + upd[...] * (h[...] - cand)
         h[...] = new
         (hb if t < LAGS - 1 else sf_o)[...] = new.astype(BF16)
@@ -281,7 +296,7 @@
     block = 0.05 * jnp.sum(soft.reshape(NBLK, BS, WIDTH), axis=1)
     btsend[...] = block.astype(BF16)
     b_moves = []
-    for k in range(1, nr):
+    for k in sorted(range(1, nr), key=lambda k: abs(2 * k - nr)):
         copy = pltpu.make_async_remote_copy(
             src_ref=btsend, dst_ref=btrecv.at[k],
             send_sem=b_send.at[k], recv_sem=b_recv.at[k],
@@ -321,11 +336,11 @@
         vmem((SEG, WIDTH), F32), vmem((SEG, WIDTH), BF16), vmem((SEG, WIDTH), BF16),
         vmem((2 * SEG, SEG + 2 * WIDTH), BF16), vmem((SEG, WIDTH), BF16), vmem((WIDTH, SEG), BF16),
         vmem((WIDTH, SEG), BF16), vmem((SEG, SEG + 2 * WIDTH), F32), vmem((WIDTH, SEG + 2 * WIDTH), BF16),
-        vmem((2 * SEG, WIDTH), F32), vmem((SEG, 2 * WIDTH), BF16), vmem((2, 2 * SEG, 2 * WIDTH), BF16),
+        vmem((SEG, 2 * WIDTH), BF16), vmem((LAGS, 2 * SEG, WIDTH), BF16),
         vmem((LAGS, SEG, 3 * WIDTH), F32), vmem((SEG, 2 * WIDTH), F32), vmem((SEG, WIDTH), F32),
-        vmem((128, 256), BF16), vmem((256, 256), BF16),
+        vmem((128, 3 * WIDTH), BF16), vmem((256, 3 * WIDTH), BF16),
         vmem((2, 128, 256), BF16), vmem((2, 256, 256), BF16),
-        vmem((2 * LAGS - 1, 128, WIDTH), BF16), vmem((2 * LAGS - 1, 256, WIDTH), BF16),
+        vmem((2 * LAGS - 1, 128, WIDTH), BF16), vmem((2 * LAGS - 1, 192, WIDTH), BF16),
         vmem((2, SLOT_HI * NBLK, WIDTH), BF16), vmem((nr, 2, own_rows, WIDTH), BF16),
         vmem((2, owned, nr * NBLK), BF16),
         vmem((NBLK, WIDTH), BF16), vmem((nr, NBLK, WIDTH), BF16),

time: 56.7 us -> 56.3 us (level)
  no operation moved by 1% of the time
where the time goes in v3:
time: 56.3 us; the launch traced here: 56.2 us
  Pallas kernels  54.2 us (96%)
  local copies, waits for them, and re-layouts  1.31 us (2%)
  between operations  0.64 us (1%)
    pallas_call x1, Pallas kernels, per_device(): call(jnp.transpose(neighbors), jnp.transpose(edge_weight), boundary.resha...  54.2 us
    unnamed x2, local copies, waits for them, and re-layouts  1.31 us

profile of v3, /device:TPU:25, one launch (start us, length us, event | category | flops | bytes accessed | tf_op | source)
XLA Modules:
  0.0 56.2 jit_solution(11280854531728204297)
XLA Ops:
  0.6 54.2 %shard_map.149 = (bf16[512,128]{1,0:T(8,128)(2,1)S(1)}, f32[256,128]{1,0:T(8,128)S(1)}) custom-call(s32[4,512]{1,0:T(4,128)} %bitcast.11, f32[4,512]{1,0:T(4,128)} %bitcast.12, s32[1,64]{1,0:T(1,128)} %bitcast.17, bf16[512,128]{1,0:T(8,128)(2,1)} %h0_h.1, bf16[512,512]{1,0:T(8,128)(2,1)} %x_h.1, bf16[3,256,256]{2,1,0:T(8,128)(2,1)} %wg_h.1, ...), custom_call_target="tpu_custom_call" | custom-call | flops 6000000000 | bytes 2000000 | tf_op jit(solution)/shard_map/pallas_call | solution.py:371
  54.9 0.7 %copy.18 = bf16[512,128]{1,0:T(8,128)(2,1)} copy(bf16[512,128]{1,0:T(8,128)(2,1)S(1)} %get-tuple-element.6) | data formatting | bytes 262144
  55.5 0.7 %copy.19 = f32[1,256,128]{2,1,0:T(8,128)} copy(f32[1,256,128]{2,1,0:T(8,128)S(1)} %bitcast.10) | data formatting | bytes 262144

commit v4 on v3

--- a/solution.py
+++ b/solution.py
@@ -42,8 +42,8 @@
     source = [valid[1], valid[0], valid[3], valid[2]]
     guests = sum(v.astype(jnp.int32) for v in valid)
 
-    def to_each(act):
-        for j in (2, 3, 0, 1):
+    def to_each(act, order=(2, 3, 0, 1)):
+        for j in order:
             pl.when(valid[j])(functools.partial(act, j, {"dom": dom + hops[j]}))
 
     peers = [None] + [lax.rem(region + k, nr) for k in range(1, nr)]
@@ -118,7 +118,7 @@
 
     sends = []
 
-    def exchange(n, src, dst, width, far_width):
+    def exchange(n, src, dst, width, far_width, between=None):
         def move(j, there):
             first, size = (0, 64)[j % 2], (64, 32)[j // 2]
             base = (0, 64, 128, 160)[j]
@@ -129,7 +129,10 @@
                 device_id=there, device_id_type=MESH,
             )
 
-        to_each(lambda j, there: move(j, there).start())
+        to_each(lambda j, there: move(j, there).start(), (2, 3))
+        if between is not None:
+            between()
+        to_each(lambda j, there: move(j, there).start(), (0, 1))
         moves = [move(j, {"dom": lax.rem(dom + 1, nd)}) for j in range(4)]
         sends.extend(enumerate(moves))
         return moves
@@ -254,8 +257,14 @@
         return dot(m[SEG:, SEG:], q)
 
     def send_field(n, field):
-        eh[n] = dot(s[...], field).astype(BF16)
-        return exchange(3 + n, eh.at[n], rh.at[n], WIDTH, WIDTH)
+        edge = dot(pk[0:64], field).astype(BF16)
+        eh[n, 0:32], eh[n, 64:96] = edge[0:32], edge[32:64]
+
+        def sums():
+            part = dot(s[...], field).astype(BF16)
+            eh[n, 32:64], eh[n, 96:128] = part[32:64], part[96:128]
+
+        return exchange(3 + n, eh.at[n], rh.at[n], WIDTH, WIDTH, sums)
 
     x_spread(0)
     x_project(0)
@@ -311,14 +320,14 @@
         for j in range(own_hi):
             part = crecv[:, plane, j * NBLK : (j + 1) * NBLK, :].reshape(nr * NBLK, WIDTH)
             ct[plane, j * WIDTH : (j + 1) * WIDTH, :] = jnp.transpose(part)
+    for j, c in sends:
+        pl.when(valid[j])(c.wait_send)
+    for c in c_moves + b_moves:
+        c.wait_send()
     for c in b_moves:
         c.wait_recv()
     times = btrecv[...].reshape(nr * NBLK, WIDTH)
     pt_o[...] = dot(ct[0], times) + dot(ct[1], times)
-    for j, c in sends:
-        pl.when(valid[j])(c.wait_send)
-    for c in c_moves + b_moves:
-        c.wait_send()
 
 
 def solution(mesh):

time: 56.3 us -> 56.3 us (level)
  no operation moved by 1% of the time
where the time goes in v4:
time: 56.3 us; the launch traced here: 56.2 us
  Pallas kernels  54.2 us (96%)
  local copies, waits for them, and re-layouts  1.31 us (2%)
  between operations  0.64 us (1%)
    pallas_call x1, Pallas kernels, per_device(): call(jnp.transpose(neighbors), jnp.transpose(edge_weight), boundary.resha...  54.2 us
    unnamed x2, local copies, waits for them, and re-layouts  1.31 us

profile of v4, /device:TPU:25, one launch (start us, length us, event | category | flops | bytes accessed | tf_op | source)
XLA Modules:
  0.0 56.2 jit_solution(8570548225165429442)
XLA Ops:
  0.6 54.2 %shard_map.149 = (bf16[512,128]{1,0:T(8,128)(2,1)S(1)}, f32[256,128]{1,0:T(8,128)S(1)}) custom-call(s32[4,512]{1,0:T(4,128)} %bitcast.11, f32[4,512]{1,0:T(4,128)} %bitcast.12, s32[1,64]{1,0:T(1,128)} %bitcast.17, bf16[512,128]{1,0:T(8,128)(2,1)} %h0_h.1, bf16[512,512]{1,0:T(8,128)(2,1)} %x_h.1, bf16[3,256,256]{2,1,0:T(8,128)(2,1)} %wg_h.1, ...), custom_call_target="tpu_custom_call" | custom-call | flops 6000000000 | bytes 2000000 | tf_op jit(solution)/shard_map/pallas_call | solution.py:380
  54.9 0.7 %copy.18 = bf16[512,128]{1,0:T(8,128)(2,1)} copy(bf16[512,128]{1,0:T(8,128)(2,1)S(1)} %get-tuple-element.6) | data formatting | bytes 262144
  55.5 0.7 %copy.19 = f32[1,256,128]{2,1,0:T(8,128)} copy(f32[1,256,128]{2,1,0:T(8,128)S(1)} %bitcast.10) | data formatting | bytes 262144
